TPU v7x, 32 devices: a whole 2x2x4 slice. The times are simulated.
32 devices in a mesh: req: 4 (over y, core), unit: 8 (over z, x).
Axes of the slice: x: 2, y: 2, z: 4, core: 2. Of those that a mesh axis runs over, the one named last changes fastest.
Arguments:
- hidden: bfloat16 [1536, 2048], P(('req', 'unit')), may hold values from -6 to 6
- tree_q: bfloat16 [1536, 2048], P(('req', 'unit')), may hold values from -1.5 to 1.5
- tree_kv: bfloat16 [1536, 2, 512], P(('req', 'unit')), may hold values from -1.5 to 1.5
- kv_cache: bfloat16 [32, 2, 2, 2048, 256], P(('req', 'unit')), may hold values from -1.5 to 1.5
- cache_lengths: int32 [32], P(('req', 'unit')), may hold values from 1 to 2048, as said below
- tree_parents: int32 [32, 48], P(('req', 'unit')), may hold values from 0 to 46, as said below
- accepted: int32 [32, 4], P(('req', 'unit')), may hold values from 0 to 47, as said below
- tenant_ranges: int32 [32, 2], replicated, may hold values from 0 to 262144, as said below
- out_weight: bfloat16 [2048, 2048], P(None, 'unit'), may hold values from -0.125 to 0.125
- mlp_weights: bfloat16 [3, 2048, 8192], P(None, None, ('req', 'unit')), may hold values from -0.125 to 0.125
- draft_weights: bfloat16 [4, 2048, 2048], P(None, None, 'unit'), may hold values from -0.125 to 0.125
- embedding: bfloat16 [262144, 2048], P(('req', 'unit')), may hold values from -1.1269514 to 1.1269514
- attn_post_gain: bfloat16 [2048], replicated, may hold values from 0.25 to 1.75
- ff_pre_gain: bfloat16 [2048], replicated, may hold values from 0.25 to 1.75
- ff_post_gain: bfloat16 [2048], replicated, may hold values from 0.25 to 1.75
- final_gain: bfloat16 [2048], replicated, may hold values from 0.25 to 1.75
Outputs:
- tree_out: bfloat16 [1536, 2048], P(('req', 'unit'))
- draft_logprobs: bfloat16 [4, 128, 262144], P(None, None, ('req', 'unit'))
Inputs may be any that keep to these rules, and one draw needn't show every extreme that they name: A request's cache holds live entries in its first cache_lengths slots; some request fills all 2048. `tree_parents`: node 0 is the root and its own parent; every other node's parent has a smaller index. `accepted`: rising nodes starting at the root 0, each the parent of the next. `tenant_ranges`: column 0 is the first allowed id, column 1 one past the last; each request allows 262144 // 2 ids or more; some request allows all.
All inputs are finite; a program needn't handle non-finite values.
Results may differ from a plain program's by a relative error of at most 0.008.
Values may be sent and summed in bfloat16 or wider, within the bound.
A program may use at most 128 MiB of HBM per device.

v0:
```python
import jax
import jax.numpy as jnp
from jax import lax
from jax.sharding import PartitionSpec as P

QH = 8
KVH = 2
HD = 256
HEADS = 4
ACC = 4


EPS = 1e-06
SOFTCAP = 30.0
BLOCK_SLOTS = 512


def rms_scale(values, gain):
    floats = values.astype(jnp.float32)
    return (
        floats
        * lax.rsqrt(jnp.mean(floats * floats, axis=-1, keepdims=True) + EPS)
        * gain.astype(jnp.float32)
    )


def ancestor_table(parents):
    tree_size = parents.shape[-1]
    node_ids = jnp.arange(tree_size, dtype=jnp.int32)
    reachable = jnp.maximum(
        (parents[:, None] == node_ids[None, :]).astype(jnp.float32),
        (node_ids[:, None] == node_ids[None, :]).astype(jnp.float32),
    )
    for doubling in range(max(1, (tree_size - 1).bit_length())):
        reachable = jnp.minimum(jnp.dot(reachable, reachable, precision=lax.Precision.HIGHEST), 1.0)
    return reachable


def cache_attention(queries, cache, length):
    slots_total = cache.shape[2]
    block_width = min(BLOCK_SLOTS, slots_total)
    blocks = slots_total // block_width
    score_scale = HD ** (-0.5)
    tree_size = queries.shape[0]
    group_size = queries.shape[2]

    def add_block(block_index, running):
        numerator, denominator = running
        offset = block_index * block_width
        key_block = lax.dynamic_slice_in_dim(cache[0], offset, block_width, 1)
        value_block = lax.dynamic_slice_in_dim(cache[1], offset, block_width, 1)
        scores = jnp.exp(
            jnp.einsum("tkgd,ksd->kgts", queries, key_block, preferred_element_type=jnp.float32)
            * score_scale
        )
        slot_ids = offset + jnp.arange(block_width, dtype=jnp.int32)
        weights_now = jnp.where(slot_ids < length, scores, 0.0)
        numerator = numerator + jnp.einsum(
            "kgts,ksd->tkgd",
            weights_now.astype(jnp.bfloat16),
            value_block,
            preferred_element_type=jnp.float32,
        )
        return (numerator, denominator + jnp.sum(weights_now, axis=3))

    start_state = (
        jnp.zeros((tree_size, KVH, group_size, HD), jnp.float32),
        jnp.zeros((KVH, group_size, tree_size), jnp.float32),
    )
    return lax.fori_loop(0, blocks, add_block, start_state)


def unit_terms(mlp_rows, weight_part):
    gate_part = jnp.dot(mlp_rows, weight_part[0], preferred_element_type=jnp.float32)
    upward = jnp.dot(mlp_rows, weight_part[1], preferred_element_type=jnp.float32)
    active = (jax.nn.gelu(gate_part, approximate=True) * upward).astype(jnp.bfloat16)
    return lax.dot_general(
        active, weight_part[2], (((1,), (1,)), ((), ())), preferred_element_type=jnp.float32
    )


def per_device(
    hidden,
    tree_q,
    tree_kv,
    kv_cache,
    cache_lengths,
    tree_parents,
    accepted,
    tenant_ranges,
    out_weight,
    mlp_weights,
    draft_weights,
    embedding,
    attn_post_gain,
    ff_pre_gain,
    ff_post_gain,
    final_gain,
):
    tree_size = tree_q.shape[0]
    group_size = QH // KVH
    queries = tree_q.reshape(tree_size, KVH, group_size, HD)
    numerator, denominator = cache_attention(queries, kv_cache[0], cache_lengths[0])
    tree_keys = tree_kv[:, 0].reshape(tree_size, KVH, HD)
    tree_values = tree_kv[:, 1].reshape(tree_size, KVH, HD)
    tree_scores = jnp.exp(
        jnp.einsum("tkgd,skd->kgts", queries, tree_keys, preferred_element_type=jnp.float32)
        * HD ** (-0.5)
    )
    tree_weights = tree_scores * ancestor_table(tree_parents[0])
    numerator = numerator + jnp.einsum(
        "kgts,skd->tkgd",
        tree_weights.astype(jnp.bfloat16),
        tree_values,
        preferred_element_type=jnp.float32,
    )
    denominator = denominator + jnp.sum(tree_weights, axis=3)
    attended = numerator / jnp.transpose(denominator, (2, 0, 1))[..., None]
    attended = attended.reshape(tree_size, QH * HD).astype(jnp.bfloat16)
    projected_cols = jnp.dot(
        lax.all_gather(attended, "unit", axis=0, tiled=True),
        out_weight,
        preferred_element_type=jnp.float32,
    ).astype(jnp.bfloat16)
    projected = lax.all_to_all(projected_cols, "unit", split_axis=0, concat_axis=1, tiled=True)
    first = (hidden.astype(jnp.float32) + rms_scale(projected, attn_post_gain)).astype(jnp.bfloat16)
    normed = rms_scale(first, ff_pre_gain).astype(jnp.bfloat16)
    mlp_rows = lax.all_gather(normed, "unit", axis=0, tiled=True)
    partial_sums = unit_terms(mlp_rows, lax.all_gather(mlp_weights, "req", axis=2, tiled=True))
    mlp_sum = lax.psum_scatter(partial_sums, "unit", scatter_dimension=0, tiled=True)
    tree_out = (first.astype(jnp.float32) + rms_scale(mlp_sum, ff_post_gain)).astype(jnp.bfloat16)
    path_rows = jnp.take(tree_out, accepted[0], axis=0)
    path_normed = rms_scale(path_rows, final_gain).astype(jnp.bfloat16)
    column_width = draft_weights.shape[2]
    column_start = lax.axis_index("unit") * column_width
    every_row = lax.all_gather(path_normed, ("req", "unit"), axis=0, tiled=True)
    before = jnp.einsum("rd,hde->rhe", every_row, draft_weights, preferred_element_type=jnp.float32)
    own_columns = lax.dynamic_slice_in_dim(every_row, column_start, column_width, 1).astype(
        jnp.float32
    )
    drafts = lax.all_gather(
        (own_columns[:, None, :] + jax.nn.silu(before)).astype(jnp.bfloat16),
        "unit",
        axis=2,
        tiled=True,
    )
    vocab_width = embedding.shape[0]
    vocab_ids = lax.axis_index(("req", "unit")) * vocab_width + jnp.arange(
        vocab_width, dtype=jnp.int32
    )
    starts = jnp.repeat(tenant_ranges[:, 0], ACC)
    range_ends = jnp.repeat(tenant_ranges[:, 1], ACC)
    allowed = (vocab_ids[None, :] >= starts[:, None]) & (vocab_ids[None, :] < range_ends[:, None])
    head_logits = []
    head_totals = []
    for head_index in range(HEADS):
        products = lax.dot_general(
            drafts[:, head_index],
            embedding,
            (((1,), (1,)), ((), ())),
            preferred_element_type=jnp.float32,
        )
        logits = SOFTCAP * jnp.tanh(products / SOFTCAP)
        head_logits.append(logits)
        head_totals.append(jnp.sum(jnp.where(allowed, jnp.exp(logits), 0.0), axis=1))
    totals = lax.psum(jnp.stack(head_totals), ("req", "unit"))
    draft_logprobs = jnp.stack(
        [
            jnp.where(allowed, head_logits[head_index] - jnp.log(totals[head_index])[:, None], 0.0)
            for head_index in range(HEADS)
        ]
    ).astype(jnp.bfloat16)
    return (tree_out, draft_logprobs)


def solution(mesh):
    return jax.shard_map(
        per_device,
        mesh=mesh,
        in_specs=(
            P(("req", "unit"), None),
            P(("req", "unit"), None),
            P(("req", "unit"), None, None),
            P(("req", "unit"), None, None, None, None),
            P(("req", "unit")),
            P(("req", "unit"), None),
            P(("req", "unit"), None),
            P(),
            P(None, "unit"),
            P(None, None, ("req", "unit")),
            P(None, None, "unit"),
            P(("req", "unit"), None),
            P(),
            P(),
            P(),
            P(),
        ),
        out_specs=(P(("req", "unit"), None), P(None, None, ("req", "unit"))),
        check_vma=False,
    )
```

profile of v0, /device:TPU:0, one launch (start us, length us, event | category | flops | bytes accessed | tf_op | source)
XLA Modules:
  0.0 563.0 jit_solution(12636101382264919844)
XLA Ops:
  11.7 16.0 %while.16 = (s32[]{:T(128)}, f32[48,2,4,256]{3,0,2,1:T(8,128)S(1)}, f32[2,4,48]{2,1,0:T(4,128)S(1)}, bf16[2,2,2048,256]{3,2,1,0:T(8,128)(2,1)}, s32[]{:T(128)}, ...) while((s32[]{:T(128)}, f32[48,2,4,256]{3,0,2,1:T(8,128)S(1)}, ...), condition=%wide.region_2.3_spmd.clone, body=%wide.region_0.2_spmd.clone.sunk | while | flops 202311040 | bytes 11214006 | solution.py:70
  12.3 2.5 fusion.102
  16.3 2.5 fusion.102
  20.3 2.5 fusion.102
  24.3 2.5 fusion.102
  29.2 47.0 %all-gather.6.cloned.1.call-done = bf16[384,2048]{1,0:T(8,128)(2,1)} async-done(((bf16[48,2048]{1,0:T(8,128)(2,1)}), bf16[384,2048]{1,0:T(8,128)(2,1)}) %all-gather.6.cloned.1.call-update) | async-done | bytes 1572880 | tf_op jit(solution)/shard_map/all_gather | solution.py:121
  76.2 2.7 convolution_convert_fusion
  78.9 3.4 all-to-all-start
  82.4 7.9 %all-to-all-done = bf16[8,48,256]{2,1,0:T(8,128)(2,1)S(1)} async-done(((bf16[8,48,256]{2,1,0:T(8,128)(2,1)}), bf16[8,48,256]{2,1,0:T(8,128)(2,1)S(1)}, u32[]{:S(2)}, u32[]{:S(2)}) %all-to-all-start) | async-done | bytes 196640 | tf_op jit(solution)/shard_map/all_to_all | solution.py:125
  92.4 42.1 %all-gather.8.cloned.1.call-done = bf16[384,2048]{1,0:T(8,128)(2,1)} async-done(((bf16[48,2048]{1,0:T(8,128)(2,1)}), bf16[384,2048]{1,0:T(8,128)(2,1)}) %all-gather.8.cloned.1.call-update) | async-done | bytes 1572880 | tf_op jit(solution)/shard_map/all_gather | solution.py:128
  134.5 84.2 %all-gather.10.cloned.1.call-done = bf16[3,2048,1024]{2,1,0:T(8,128)(2,1)} async-done(((bf16[3,2048,256]{2,1,0:T(8,128)(2,1)}), bf16[3,2048,1024]{2,1,0:T(8,128)(2,1)}) %all-gather.10.cloned.1.call-update) | async-done | bytes 12582928 | tf_op jit(solution)/shard_map/all_gather | solution.py:129
  218.7 5.6 fusion.21
  224.3 9.2 %fusion.19 = f32[384,2048]{1,0:T(8,128)} fusion(bf16[3,2048,1024]{2,1,0:T(8,128)(2,1)} %all-gather.10.cloned.1.call-done, f32[384,1024]{1,0:T(8,128)} %fusion.21, bf16[384,2048]{1,0:T(8,128)(2,1)S(1)} %copy-done.10), kind=kOutput, calls=%fused_computation.30 | convolution fusion | flops 3225157632 | bytes 14680064 | tf_op jit(solution)/shard_map/dot_general | solution.py:77
  233.6 74.2 %reduce-scatter.2.cloned.1.call-done = f32[48,2048]{1,0:T(8,128)} async-done(((f32[384,2048]{1,0:T(8,128)}), f32[48,2048]{1,0:T(8,128)}) %reduce-scatter.2.cloned.1.call-update) | async-done | bytes 393232 | tf_op jit(solution)/shard_map/reduce_scatter | solution.py:130
  311.0 69.1 %all-gather = bf16[32,4,2048]{2,1,0:T(4,128)(2,1)S(1)} all-gather(bf16[1,4,2048]{2,1,0:T(4,128)(2,1)S(1)} %fusion.59), channel_id=1, replica_groups=mesh['req'=4,'unit'=8] {'req','unit'}, dimensions={0}, use_global_device_ids=true | all-gather | bytes 540672 | tf_op jit(solution)/shard_map/all_gather | solution.py:136
  380.4 3.7 add_convert_fusion
  384.5 46.9 %all-gather.12.cloned.1.call-done = bf16[128,4,2048]{2,0,1:T(8,128)(2,1)} async-done(((bf16[128,4,256]{2,0,1:T(8,128)(2,1)}), bf16[128,4,2048]{2,0,1:T(8,128)(2,1)}) %all-gather.12.cloned.1.call-update) | async-done | bytes 2097168 | tf_op jit(solution)/shard_map/all_gather | solution.py:141
  431.5 18.0 %fusion.18 = f32[128,8192]{1,0:T(8,128)} fusion(bf16[8192,2048]{1,0:T(8,128)(2,1)} %param.29, bf16[128,4,2048]{2,0,1:T(8,128)(2,1)} %all-gather.12.cloned.1.call-done), kind=kOutput, calls=%fused_computation.27 | convolution fusion | flops 4297064448 | bytes 38273024 | tf_op jit(solution)/shard_map/dot_general | solution.py:157
  449.5 17.9 %fusion.17 = f32[128,8192]{1,0:T(8,128)} fusion(bf16[8192,2048]{1,0:T(8,128)(2,1)} %param.29, bf16[128,4,2048]{2,0,1:T(8,128)(2,1)S(1)} %copy-done.2), kind=kOutput, calls=%fused_computation.26 | convolution fusion | flops 4297064448 | bytes 38273024 | tf_op jit(solution)/shard_map/dot_general | solution.py:157
  467.4 18.0 %fusion.16 = f32[128,8192]{1,0:T(8,128)} fusion(bf16[8192,2048]{1,0:T(8,128)(2,1)} %param.29, bf16[128,4,2048]{2,0,1:T(8,128)(2,1)S(1)} %copy-done.2), kind=kOutput, calls=%fused_computation.25 | convolution fusion | flops 4297064448 | bytes 38273024 | tf_op jit(solution)/shard_map/dot_general | solution.py:157
  485.4 21.6 %select_reduce_fusion.3 = (f32[128]{0:T(128)S(1)}, f32[128]{0:T(128)S(1)}, f32[128]{0:T(128)S(1)}, f32[128]{0:T(128)S(1)}, f32[128,8192]{1,0:T(8,128)}) fusion(s32[128]{0:T(128)S(1)} %lt.58, s32[128]{0:T(128)S(1)} %ge.23, s32[8192]{0:T(1024)S(1)} %iota_add_fusion, f32[128,8192]{1,0:T(8,128)} %fusion.16, f32[128,8192]{1,0:T(8,128)} %fusion.17, ...), kind=kOutput, calls=%fused_computation.42 | convolution fusion | flops 4308598784 | bytes 50891776 | tf_op jit(solution)/shard_map/dot_general | solution.py:157
  507.0 38.4 %psum.7 = f32[4,128]{1,0:T(4,128)S(1)} all-reduce(f32[4,128]{1,0:T(4,128)S(1)} %pad_maximum_fusion.1), channel_id=1, replica_groups=mesh['req'=4,'unit'=8] {'req','unit'}, use_global_device_ids=true, to_apply=%region_13.14 | all-reduce | flops 512 | bytes 4096 | tf_op jit(solution)/shard_map/psum | solution.py:166
  545.4 7.1 %fusion.22 = (bf16[1,128,8192]{2,1,0:T(8,128)(2,1)S(1)}, bf16[1,128,8192]{2,1,0:T(8,128)(2,1)S(1)}, bf16[1,128,8192]{2,1,0:T(8,128)(2,1)S(1)}, bf16[1,128,8192]{2,1,0:T(8,128)(2,1)S(1)}) fusion(f32[128,8192]{1,0:T(8,128)} %get-tuple-element.183, f32[128]{0:T(128)S(1)} %get-tuple-element.175, s32[128]{0:T(128)S(1)} %lt.58, s32[128]{0:T(128)S(1)} %ge.23, ...), kind=kLoop, calls=%fused_computation.45 | loop fusion | flops 15728640 | bytes 25201664 | tf_op jit(solution)/shard_map/stack | solution.py:167
  552.6 3.9 pad_maximum_fusion
  (101 shorter events, 17.7 us)
Async XLA Ops:
  7.2 69.0 %copy-start = (bf16[2048,256]{1,0:T(8,128)(2,1)S(1)}, bf16[2048,256]{1,0:T(8,128)(2,1)}, u32[]{:S(2)}) copy-start(bf16[2048,256]{1,0:T(8,128)(2,1)} %param.26) | copy-start | bytes 3145732
  7.2 69.0 %all-gather.6.cloned.1.call-start = ((), (), s32[]{:S(2)}) async-start(), calls=%async_computation.2 | async-start | bytes 1769472 | tf_op jit(solution)/shard_map/all_gather | solution.py:121
  27.6 54.7 %copy-start.5 = (bf16[2048]{0:T(1024)(128)(2,1)S(1)}, bf16[2048]{0:T(1024)(128)(2,1)}, u32[]{:S(2)}) copy-start(bf16[2048]{0:T(1024)(128)(2,1)} %param.30) | copy-start | bytes 12292
  27.7 54.7 %copy-start.6 = (bf16[2048]{0:T(1024)(128)(2,1)S(1)}, bf16[2048]{0:T(1024)(128)(2,1)}, u32[]{:S(2)}) copy-start(bf16[2048]{0:T(1024)(128)(2,1)} %param.31) | copy-start | bytes 12292
  27.9 62.5 %copy-start.4 = (bf16[48,2048]{1,0:T(8,128)(2,1)S(1)}, bf16[48,2048]{1,0:T(8,128)(2,1)}, u32[]{:S(2)}) copy-start(bf16[48,2048]{1,0:T(8,128)(2,1)} %param.18) | copy-start | bytes 589828
  78.9 11.4 %all-to-all-start = ((bf16[8,48,256]{2,1,0:T(8,128)(2,1)}), bf16[8,48,256]{2,1,0:T(8,128)(2,1)S(1)}, u32[]{:S(2)}, u32[]{:S(2)}) async-start(bf16[8,48,256]{2,1,0:T(8,128)(2,1)} %bitcast.8), calls=%async_computation | async-start | bytes 393216 | tf_op jit(solution)/shard_map/all_to_all | solution.py:125
  82.3 52.2 %all-gather.8.cloned.1.call-start = ((), (), s32[]{:S(2)}) async-start(), calls=%async_computation.3 | async-start | bytes 1769472 | tf_op jit(solution)/shard_map/all_gather | solution.py:128
  91.6 127.1 %all-gather.10.cloned.1.call-start = ((), (), s32[]{:S(2)}) async-start(), calls=%async_computation.4 | async-start | bytes 15728640 | tf_op jit(solution)/shard_map/all_gather | solution.py:129
  92.3 215.5 %reduce-scatter.2.cloned.1.call-start = ((), (), s32[]{:S(2)}) async-start(), calls=%async_computation.5 | async-start | bytes 3538944 | tf_op jit(solution)/shard_map/reduce_scatter | solution.py:130
  134.5 89.8 %copy-start.10 = (bf16[384,2048]{1,0:T(8,128)(2,1)S(1)}, bf16[384,2048]{1,0:T(8,128)(2,1)}, u32[]{:S(2)}) copy-start(bf16[384,2048]{1,0:T(8,128)(2,1)} %all-gather.8.cloned.1.call-done) | copy-start | bytes 4718596
  224.2 9.3 %copy-start.7 = (bf16[2048]{0:T(1024)(128)(2,1)S(1)}, bf16[2048]{0:T(1024)(128)(2,1)}, u32[]{:S(2)}) copy-start(bf16[2048]{0:T(1024)(128)(2,1)} %param.32) | copy-start | bytes 12292
  224.3 9.3 %copy-start.8 = (bf16[2048]{0:T(1024)(128)(2,1)S(1)}, bf16[2048]{0:T(1024)(128)(2,1)}, u32[]{:S(2)}) copy-start(bf16[2048]{0:T(1024)(128)(2,1)} %param.33) | copy-start | bytes 12292
  224.3 9.3 %copy-start.11 = (s32[1,4]{1,0:T(1,128)S(1)}, s32[1,4]{1,0:T(1,128)}, u32[]{:S(2)}) copy-start(s32[1,4]{1,0:T(1,128)} %param.24) | copy-start | bytes 52
  233.5 198.0 %all-gather.12.cloned.1.call-start = ((), (), s32[]{:S(2)}) async-start(), calls=%async_computation.6 | async-start | bytes 2359296 | tf_op jit(solution)/shard_map/all_gather | solution.py:141
  310.1 74.0 %copy-start.3 = (bf16[48,2048]{1,0:T(8,128)(2,1)}, bf16[48,2048]{1,0:T(8,128)(2,1)S(1)}, u32[]{:S(2)}) copy-start(bf16[48,2048]{1,0:T(8,128)(2,1)S(1)} %fusion.49) | copy-start | bytes 589828
  380.2 3.9 copy-start.9
  431.5 18.0 %copy-start.2 = (bf16[128,4,2048]{2,0,1:T(8,128)(2,1)S(1)}, bf16[128,4,2048]{2,0,1:T(8,128)(2,1)}, u32[]{:S(2)}) copy-start(bf16[128,4,2048]{2,0,1:T(8,128)(2,1)} %all-gather.12.cloned.1.call-done) | copy-start | bytes 6291460
  552.5 3.9 copy-start.1
Sparse Core Ops, SparseCore 0:
  29.3 46.8 all-gather.5
  91.7 42.7 all-gather.7
  136.0 82.5 all-gather.9
  233.6 74.1 reduce-scatter.1
  384.2 47.1 all-gather.11
where the time goes:
time: 564 us; the launch traced here: 563 us
  waiting for transfers between devices  303 us (54%)
  blocking collectives  108 us (19%)
  matrix products  102 us (18%)
  other arithmetic  17.5 us (3%)
  local copies, waits for them, and re-layouts  14.8 us (3%)
  between operations  14.2 us (3%)
    all_gather x1, waiting for transfers between devices, per_device(): lax.all_gather(mlp_weights, 'req', axis=2, tiled=True)  84.2 us
    dot_general x4, matrix products, per_device(): lax.dot_general(drafts[:, head_index], embedding, (((1,), (1,)), ((), ())...  75.5 us
    reduce_scatter x1, waiting for transfers between devices, per_device(): lax.psum_scatter(partial_sums, 'unit', scatter_dimension=0, tiled=True)  74.2 us
    all_gather x1, blocking collectives, per_device(): every_row = lax.all_gather(path_normed, ('req', 'unit'), axis=0, tiled=True)  69.1 us
    all_gather x1, waiting for transfers between devices, per_device(): lax.all_gather(attended, 'unit', axis=0, tiled=True)  47 us
    all_gather x1, waiting for transfers between devices, per_device(): lax.all_gather((own_columns[:, None, :] + jax.nn.silu(before)).astype(jnp...  46.9 us
    all_gather x1, waiting for transfers between devices, per_device(): mlp_rows = lax.all_gather(normed, 'unit', axis=0, tiled=True)  42.1 us
    psum x1, blocking collectives, per_device(): totals = lax.psum(jnp.stack(head_totals), ('req', 'unit'))  38.4 us
  transfers between devices with their start and end apart: 6, of which 6 were waited for; matrix products, arithmetic and copies ran while one was open for 0% of the time, Pallas kernels for 0%

commit v1 on v0

v1 whole, which is shorter than its diff:
```python
import functools

import jax
import jax.numpy as jnp
from jax import lax
from jax.experimental import pallas as pl
from jax.experimental.pallas import tpu as pltpu
from jax.sharding import PartitionSpec as P

QH = 8
KVH = 2
HD = 256
HEADS = 4
ACC = 4

EPS = 1e-06
SOFTCAP = 30.0
MIB = 1024 * 1024
NT = (((1,), (1,)), ((), ()))


def rms_scale(values, gain):
    floats = values.astype(jnp.float32)
    return (
        floats
        * lax.rsqrt(jnp.mean(floats * floats, axis=-1, keepdims=True) + EPS)
        * gain.astype(jnp.float32)
    )


def dot_nt(left, right):
    return lax.dot_general(left, right, NT, preferred_element_type=jnp.float32)


def attention_kernel(length_ref, parents_ref, q_ref, tk_ref, tv_ref, cache_ref, out_ref):
    tree = q_ref.shape[0]
    group = QH // KVH
    slots = cache_ref.shape[3]
    width = min(512, slots)
    scale = HD ** (-0.5)
    length = length_ref[0]
    node = lax.broadcasted_iota(jnp.int32, (tree, tree), 0)
    other = lax.broadcasted_iota(jnp.int32, (tree, tree), 1)
    eye = jnp.where(node == other, 1.0, 0.0)
    parent = jnp.broadcast_to(parents_ref[...], (tree, tree))
    below = jnp.maximum(jnp.where(parent == node, 1.0, 0.0), eye)
    for _ in range(max(1, (tree - 1).bit_length())):
        bits = below.astype(jnp.bfloat16)
        below = jnp.minimum(jnp.dot(bits, bits, preferred_element_type=jnp.float32), 1.0)
    ancestor = lax.dot_general(
        below.astype(jnp.bfloat16),
        eye.astype(jnp.bfloat16),
        (((0,), (0,)), ((), ())),
        preferred_element_type=jnp.float32,
    )
    queries = jnp.concatenate([q_ref[:, g * HD : (g + 1) * HD] for g in range(group)], axis=0)
    weights = jnp.exp(dot_nt(queries, tk_ref[...]) * scale) * jnp.concatenate([ancestor] * group, 0)
    total = jnp.sum(weights, axis=1, keepdims=True)
    number = jnp.dot(
        weights.astype(jnp.bfloat16), tv_ref[...], preferred_element_type=jnp.float32
    )
    for block in range(slots // width):
        span = slice(block * width, (block + 1) * width)
        scores = jnp.exp(dot_nt(queries, cache_ref[0, 0, 0, span, :]) * scale)
        slot = block * width + lax.broadcasted_iota(jnp.int32, scores.shape, 1)
        weights = jnp.where(slot < length, scores, 0.0)
        total = total + jnp.sum(weights, axis=1, keepdims=True)
        number = number + jnp.dot(
            weights.astype(jnp.bfloat16),
            cache_ref[0, 1, 0, span, :],
            preferred_element_type=jnp.float32,
        )
    result = (number / total).astype(jnp.bfloat16)
    for g in range(group):
        out_ref[:, g * HD : (g + 1) * HD] = result[g * tree : (g + 1) * tree, :]


def attend(tree_q, tree_kv, kv_cache, cache_lengths, tree_parents):
    tree = tree_q.shape[0]
    slots = kv_cache.shape[3]
    wide = QH // KVH * HD
    return pl.pallas_call(
        attention_kernel,
        grid=(KVH,),
        out_shape=jax.ShapeDtypeStruct((tree, QH * HD), jnp.bfloat16),
        in_specs=[
            pl.BlockSpec(memory_space=pltpu.SMEM),
            pl.BlockSpec((1, tree), lambda k: (0, 0)),
            pl.BlockSpec((tree, wide), lambda k: (0, k)),
            pl.BlockSpec((tree, HD), lambda k: (0, k)),
            pl.BlockSpec((tree, HD), lambda k: (0, k)),
            pl.BlockSpec((1, 2, 1, slots, HD), lambda k: (0, 0, k, 0, 0)),
        ],
        out_specs=pl.BlockSpec((tree, wide), lambda k: (0, k)),
        compiler_params=pltpu.CompilerParams(vmem_limit_bytes=24 * MIB),
        cost_estimate=pl.CostEstimate(
            flops=4 * tree * QH * HD * slots,
            bytes_accessed=8 * slots * KVH * HD,
            transcendentals=tree * QH * slots,
        ),
        name="tree_attention",
    )(cache_lengths, tree_parents, tree_q, tree_kv[:, 0], tree_kv[:, 1], kv_cache)


def draft_kernel(rows_ref, weight_ref, out_ref):
    width = weight_ref.shape[2]
    start = pl.multiple_of(lax.axis_index("unit") * width, width)
    before = jnp.dot(rows_ref[...], weight_ref[0], preferred_element_type=jnp.float32)
    own = rows_ref[:, pl.ds(start, width)].astype(jnp.float32)
    out_ref[0] = (own + before * jax.nn.sigmoid(before)).astype(jnp.bfloat16)


def draft_columns(rows, draft_weights):
    count, depth = rows.shape
    heads, _, width = draft_weights.shape
    return pl.pallas_call(
        draft_kernel,
        grid=(heads,),
        out_shape=jax.ShapeDtypeStruct((heads, count, width), jnp.bfloat16),
        in_specs=[
            pl.BlockSpec((count, depth), lambda h: (0, 0)),
            pl.BlockSpec((1, depth, width), lambda h: (h, 0, 0)),
        ],
        out_specs=pl.BlockSpec((1, count, width), lambda h: (h, 0, 0)),
        compiler_params=pltpu.CompilerParams(vmem_limit_bytes=24 * MIB),
        cost_estimate=pl.CostEstimate(
            flops=2 * heads * count * depth * width,
            bytes_accessed=2 * heads * depth * width,
            transcendentals=heads * count * width,
        ),
        name="draft_heads",
    )(rows, draft_weights)


def allowed_ids(start, end, first_id, shape):
    ids = first_id + lax.broadcasted_iota(jnp.int32, shape, 1)
    return (ids >= start) & (ids < end)


def logits_kernel(chunk, drafts_ref, emb_ref, start_ref, end_ref, logits_ref, sums_ref, rows_ref):
    step = pl.program_id(0)
    blocks, count, width = drafts_ref.shape
    tile = emb_ref.shape[0]
    vocab = tile * pl.num_programs(0)
    first_id = (lax.axis_index("req") * lax.axis_size("unit") + lax.axis_index("unit")) * vocab

    @pl.when(step == 0)
    def _():
        for b in range(blocks):
            rows_ref[:, b * width : (b + 1) * width] = drafts_ref[b]
        sums_ref[...] = jnp.zeros_like(sums_ref)

    start, end = start_ref[...], end_ref[...]
    for c in range(tile // chunk):
        span = slice(c * chunk, (c + 1) * chunk)
        products = dot_nt(rows_ref[...], emb_ref[span, :])
        logits = SOFTCAP * jnp.tanh(products * (1.0 / SOFTCAP))
        logits_ref[:, span] = logits
        keep = allowed_ids(start, end, first_id + step * tile + c * chunk, logits.shape)
        terms = jnp.where(keep, jnp.exp(logits), 0.0)
        part = terms[:, :128]
        for lane in range(128, chunk, 128):
            part = part + terms[:, lane : lane + 128]
        sums_ref[...] += part


def finish_kernel(logits_ref, logs_ref, start_ref, end_ref, out_ref):
    tile = logits_ref.shape[1]
    vocab = tile * pl.num_programs(0)
    first_id = (lax.axis_index("req") * lax.axis_size("unit") + lax.axis_index("unit")) * vocab
    keep = allowed_ids(
        start_ref[...], end_ref[...], first_id + pl.program_id(0) * tile, logits_ref.shape
    )
    values = jnp.where(keep, logits_ref[...] - logs_ref[...], 0.0).astype(jnp.bfloat16)
    out_ref[...] = values.reshape(out_ref.shape)


def vocabulary(drafts, embedding, tenant_ranges):
    blocks, count, width = drafts.shape
    vocab, depth = embedding.shape
    rows = count // HEADS
    bounds = jnp.tile(jnp.repeat(tenant_ranges, ACC, axis=0), (HEADS, 1))
    starts, ends = bounds[:, :1], bounds[:, 1:]
    tile = min(1024, vocab, MIB // 2 // count)
    once = pl.BlockSpec((count, 1), lambda i: (0, 0))
    logits, sums = pl.pallas_call(
        functools.partial(logits_kernel, min(256, tile)),
        grid=(vocab // tile,),
        out_shape=(
            jax.ShapeDtypeStruct((count, vocab), jnp.float32),
            jax.ShapeDtypeStruct((count, 128), jnp.float32),
        ),
        in_specs=[
            pl.BlockSpec((blocks, count, width), lambda i: (0, 0, 0)),
            pl.BlockSpec((tile, depth), lambda i: (i, 0)),
            once,
            once,
        ],
        out_specs=(
            pl.BlockSpec((count, tile), lambda i: (0, i)),
            pl.BlockSpec((count, 128), lambda i: (0, 0)),
        ),
        scratch_shapes=[pltpu.VMEM((count, depth), jnp.bfloat16)],
        compiler_params=pltpu.CompilerParams(vmem_limit_bytes=56 * MIB),
        cost_estimate=pl.CostEstimate(
            flops=2 * count * depth * vocab,
            bytes_accessed=2 * depth * vocab + 4 * count * vocab,
            transcendentals=2 * count * vocab,
        ),
        name="vocabulary_logits",
    )(drafts, embedding, starts, ends)
    totals = lax.psum(jnp.sum(sums, axis=1), ("req", "unit"))
    return pl.pallas_call(
        finish_kernel,
        grid=(vocab // tile,),
        out_shape=jax.ShapeDtypeStruct((HEADS, rows, vocab), jnp.bfloat16),
        in_specs=[pl.BlockSpec((count, tile), lambda i: (0, i)), once, once, once],
        out_specs=pl.BlockSpec((HEADS, rows, tile), lambda i: (0, 0, i)),
        compiler_params=pltpu.CompilerParams(vmem_limit_bytes=40 * MIB),
        cost_estimate=pl.CostEstimate(
            flops=2 * count * vocab, bytes_accessed=6 * count * vocab, transcendentals=0
        ),
        name="log_probabilities",
    )(logits, jnp.log(totals)[:, None], starts, ends)


def unit_terms(mlp_rows, weight_part):
    gate_part = jnp.dot(mlp_rows, weight_part[0], preferred_element_type=jnp.float32)
    upward = jnp.dot(mlp_rows, weight_part[1], preferred_element_type=jnp.float32)
    active = (jax.nn.gelu(gate_part, approximate=True) * upward).astype(jnp.bfloat16)
    return dot_nt(active, weight_part[2])


def project_rows(attended, out_weight):
    cols = jnp.dot(
        lax.all_gather(attended, "unit", axis=0, tiled=True),
        out_weight,
        preferred_element_type=jnp.float32,
    ).astype(jnp.bfloat16)
    return lax.all_to_all(cols, "unit", split_axis=0, concat_axis=1, tiled=True)


def per_device(
    hidden,
    tree_q,
    tree_kv,
    kv_cache,
    cache_lengths,
    tree_parents,
    accepted,
    tenant_ranges,
    out_weight,
    mlp_weights,
    draft_weights,
    embedding,
    attn_post_gain,
    ff_pre_gain,
    ff_post_gain,
    final_gain,
):
    group_weights = lax.all_gather(mlp_weights, "req", axis=2, tiled=True)
    attended = attend(tree_q, tree_kv, kv_cache, cache_lengths, tree_parents)

    def after_attention(residual, projected):
        first = (residual.astype(jnp.float32) + rms_scale(projected, attn_post_gain)).astype(
            jnp.bfloat16
        )
        return first, rms_scale(first, ff_pre_gain).astype(jnp.bfloat16)

    def after_mlp(first, mlp_sum):
        return (first.astype(jnp.float32) + rms_scale(mlp_sum, ff_post_gain)).astype(jnp.bfloat16)

    path_attended = jnp.take(attended, accepted[0], axis=0)
    path_hidden = jnp.take(hidden, accepted[0], axis=0)
    path_first, path_mlp_rows = after_attention(
        path_hidden, project_rows(path_attended, out_weight)
    )
    partial = unit_terms(
        lax.all_gather(path_mlp_rows, ("req", "unit"), axis=0, tiled=True), mlp_weights
    )
    path_sum = lax.psum_scatter(partial, ("req", "unit"), scatter_dimension=0, tiled=True)
    path_normed = rms_scale(after_mlp(path_first, path_sum), final_gain).astype(jnp.bfloat16)
    every_row = lax.all_gather(path_normed, ("req", "unit"), axis=0, tiled=True)
    own = draft_columns(every_row, draft_weights)
    own = own.reshape(own.shape[0] * own.shape[1], own.shape[2])
    drafts = lax.all_gather(own, "unit", axis=0)
    draft_logprobs = vocabulary(drafts, embedding, tenant_ranges)

    first, normed = after_attention(hidden, project_rows(attended, out_weight))
    mlp_rows = lax.all_gather(normed, "unit", axis=0, tiled=True)
    partial_sums = unit_terms(mlp_rows, group_weights)
    mlp_sum = lax.psum_scatter(partial_sums, "unit", scatter_dimension=0, tiled=True)
    return (after_mlp(first, mlp_sum), draft_logprobs)


def solution(mesh):
    return jax.shard_map(
        per_device,
        mesh=mesh,
        in_specs=(
            P(("req", "unit"), None),
            P(("req", "unit"), None),
            P(("req", "unit"), None, None),
            P(("req", "unit"), None, None, None, None),
            P(("req", "unit")),
            P(("req", "unit"), None),
            P(("req", "unit"), None),
            P(),
            P(None, "unit"),
            P(None, None, ("req", "unit")),
            P(None, None, "unit"),
            P(("req", "unit"), None),
            P(),
            P(),
            P(),
            P(),
        ),
        out_specs=(P(("req", "unit"), None), P(None, None, ("req", "unit"))),
        check_vma=False,
    )
```

time: 564 us -> 545 us (0.966)
  blocking collectives: 108 us -> 207 us
  waiting for transfers between devices: 303 us -> 222 us
  matrix products: 102 us -> 22.8 us
  Pallas kernels: 0 us -> 46.9 us
  other arithmetic: 17.5 us -> 7.96 us
  starting transfers between devices: 3.61 us -> 9.5 us
    unnamed x5 -> x7, waiting for transfers between devices: 0.75 us -> 183 us
    all_gather x3, waiting for transfers between devices: 178 us -> 29.8 us  [the longest x1 29.8 us: per_device(): drafts = lax.all_gather(own, 'unit', axis=0)]
    all_gather x0 -> x2, blocking collectives: none -> 99 us  [the longest x1 66.6 us: per_device(): lax.all_gather(path_mlp_rows, ('req', 'unit'), axis=0, tiled=True)]
    dot_general x23 -> x4, matrix products: 96.5 us -> 15.5 us  [the longest x2 12.6 us: dot_nt(): return lax.dot_general(left, right, NT, preferred_element_type=jnp.float32)]
    reduce_scatter x1, waiting for transfers between devices: 74.2 us -> 0.01 us  [per_device(): lax.psum_scatter(partial_sums, 'unit', scatter_dimension=0, tiled=True)]
    pallas_call x0 -> x4, Pallas kernels: none -> 46.9 us  [the longest x1 27.7 us: vocabulary(): pl.pallas_call(functools.partial(logits_kernel, min(256, tile)), grid=(vo...]
    all_gather x1, waiting for transfers between devices: 42.1 us -> 0.02 us  [per_device(): mlp_rows = lax.all_gather(normed, 'unit', axis=0, tiled=True)]
    another operation x3 -> x0, other arithmetic: 11 us -> none  [the longest x2 11 us: per_device(): jnp.stack([jnp.where(allowed, head_logits[head_index] - jnp.log(totals[he...]
  transfers between devices with their start and end apart: 6 -> 8, of which waited for: 6 -> 4; matrix products, arithmetic and copies ran while one was open for 0% -> 5% of each run, Pallas kernels for 0% -> 8%
where the time goes in v1:
time: 545 us; the launch traced here: 544 us
  waiting for transfers between devices  222 us (41%)
  blocking collectives  207 us (38%)
  Pallas kernels  46.9 us (9%)
  matrix products  22.8 us (4%)
  between operations  16.3 us (3%)
  local copies, waits for them, and re-layouts  12.1 us (2%)
  starting transfers between devices  9.5 us (2%)
  other arithmetic  7.96 us (1%)
    unnamed x7, waiting for transfers between devices  183 us
    all_gather x1, blocking collectives, per_device(): every_row = lax.all_gather(path_normed, ('req', 'unit'), axis=0, tiled=True)  68.1 us
    all_gather x1, blocking collectives, per_device(): lax.all_gather(path_mlp_rows, ('req', 'unit'), axis=0, tiled=True)  66.6 us
    psum x1, blocking collectives, vocabulary(): totals = lax.psum(jnp.sum(sums, axis=1), ('req', 'unit'))  39.6 us
    all_gather x1, blocking collectives, project_rows(): lax.all_gather(attended, 'unit', axis=0, tiled=True)  32.4 us
    all_gather x1, waiting for transfers between devices, per_device(): drafts = lax.all_gather(own, 'unit', axis=0)  29.8 us
    pallas_call x1, Pallas kernels, vocabulary(): pl.pallas_call(functools.partial(logits_kernel, min(256, tile)), grid=(vo...  27.7 us
    pallas_call x1, Pallas kernels, vocabulary(): pl.pallas_call(finish_kernel, grid=(vocab // tile,), out_shape=jax.ShapeD...  12.8 us
  transfers between devices with their start and end apart: 8, of which 4 were waited for; matrix products, arithmetic and copies ran while one was open for 5% of the time, Pallas kernels for 8%

profile of v1, /device:TPU:0, one launch (start us, length us, event | category | flops | bytes accessed | tf_op | source)
XLA Modules:
  0.0 543.9 jit_solution(4960453907976372546)
XLA Ops:
  8.8 1.1 fusion.56
  10.0 2.2 copy-done.2
  13.7 4.2 tree_attention.1
  18.0 1.6 gather_fusion.1
  19.7 32.4 %all-gather = bf16[8,4,2048]{2,1,0:T(4,128)(2,1)S(1)} all-gather(bf16[1,4,2048]{2,1,0:T(4,128)(2,1)S(1)} %select_bitcast_fusion), channel_id=1, replica_groups=mesh['req'=4,'unit'=8] {'unit'}, dimensions={0}, use_global_device_ids=true | all-gather | bytes 147456 | tf_op jit(solution)/shard_map/all_gather | solution.py:236
  53.1 5.7 %all-to-all-start.1 = ((bf16[8,4,256]{2,1,0:T(4,128)(2,1)}), bf16[8,4,256]{2,1,0:T(4,128)(2,1)S(1)}, u32[]{:S(2)}, u32[]{:S(2)}) async-start(bf16[8,4,256]{2,1,0:T(4,128)(2,1)} %all_to_all.22), calls=%async_computation.2 | async-start | bytes 32768 | tf_op jit(solution)/shard_map/all_to_all | solution.py:240
  59.4 6.1 %all-to-all-done.1 = bf16[8,4,256]{2,1,0:T(4,128)(2,1)S(1)} async-done(((bf16[8,4,256]{2,1,0:T(4,128)(2,1)}), bf16[8,4,256]{2,1,0:T(4,128)(2,1)S(1)}, u32[]{:S(2)}, u32[]{:S(2)}) %all-to-all-start.1) | async-done | bytes 16416 | tf_op jit(solution)/shard_map/all_to_all | solution.py:240
  66.0 66.6 %all-gather.1 = bf16[32,4,2048]{2,1,0:T(4,128)(2,1)S(1)} all-gather(bf16[1,4,2048]{2,1,0:T(4,128)(2,1)S(1)} %fusion.48), channel_id=1, replica_groups=mesh['req'=4,'unit'=8] {'req','unit'}, dimensions={0}, use_global_device_ids=true | all-gather | bytes 540672 | tf_op jit(solution)/shard_map/all_gather | solution.py:279
  132.7 2.7 convolution_convert_fusion
  135.4 3.4 all-to-all-start
  138.8 1.6 fusion.38
  140.4 3.4 fusion.13
  143.9 2.6 all-to-all-done
  148.7 182.3 %all-reduce.3.cloned.1.call-done = f32[128,2048]{1,0:T(8,128)} async-done(((f32[128,2048]{1,0:T(8,128)}), f32[128,2048]{1,0:T(8,128)}) %all-reduce.3.cloned.1.call-update) | async-done | bytes 1048592
  333.1 68.1 %all-gather.2 = bf16[32,4,2048]{2,1,0:T(4,128)(2,1)S(1)} all-gather(bf16[1,4,2048]{2,1,0:T(4,128)(2,1)S(1)} %fusion.49), channel_id=1, replica_groups=mesh['req'=4,'unit'=8] {'req','unit'}, dimensions={0}, use_global_device_ids=true | all-gather | bytes 540672 | tf_op jit(solution)/shard_map/all_gather | solution.py:283
  401.3 2.2 copy-done.3
  403.5 2.2 draft_heads.1
  406.1 5.7 %fusion.2 = f32[384,1024]{1,0:T(8,128)} fusion(bf16[384,2048]{1,0:T(8,128)(2,1)} %all-gather.10.cloned.1.call-done, bf16[3,2048,1024]{2,1,0:T(8,128)(2,1)} %all-gather.12.cloned.1.call-done), kind=kOutput, calls=%fused_computation.7 | convolution fusion | flops 1610612736 | bytes 7340032 | tf_op jit(solution)/shard_map/dot_general | solution.py:228
  411.8 9.2 %fusion = f32[384,2048]{1,0:T(8,128)} fusion(bf16[3,2048,1024]{2,1,0:T(8,128)(2,1)} %all-gather.12.cloned.1.call-done, f32[384,1024]{1,0:T(8,128)} %fusion.2, bf16[384,2048]{1,0:T(8,128)(2,1)S(1)} %copy-done.14), kind=kOutput, calls=%fused_computation.3 | convolution fusion | flops 3225157632 | bytes 14680064 | tf_op jit(solution)/shard_map/dot_general | solution.py:32
  422.6 29.8 %all-gather.14.cloned.1.call-done.drafts_ref = bf16[8,512,256]{2,1,0:T(8,128)(2,1)} async-done(((bf16[1,512,256]{2,1,0:T(8,128)(2,1)}), bf16[8,512,256]{2,1,0:T(8,128)(2,1)}) %all-gather.14.cloned.1.call-update) | async-done | bytes 2097168 | tf_op jit(solution)/shard_map/all_gather | solution.py:286
  452.4 27.7 %vocabulary_logits.1 = (f32[512,8192]{1,0:T(8,128)}, f32[512,128]{1,0:T(8,128)}) custom-call(bf16[8,512,256]{2,1,0:T(8,128)(2,1)} %all-gather.14.cloned.1.call-done.drafts_ref, bf16[8192,2048]{1,0:T(8,128)(2,1)} %emb_ref.1, s32[512,1]{1,0:T(8,128)} %get-tuple-element.14.start_ref, s32[512,1]{1,0:T(8,128)} %get-tuple-element.13.end_ref), custom_call_target="tpu_custom_call" | custom-call | flops 17179869184 | bytes 50331648 | tf_op jit(solution)/shard_map/vocabulary_logits/pallas_call | solution.py:186
  481.2 39.6 %psum.7 = f32[512]{0:T(512)S(1)} all-reduce(f32[512]{0:T(512)S(1)} %reduce_sum.79), channel_id=1, replica_groups=mesh['req'=4,'unit'=8] {'req','unit'}, use_global_device_ids=true, to_apply=%region_10.12 | all-reduce | flops 512 | bytes 4096 | tf_op jit(solution)/shard_map/psum | solution.py:212
  521.0 12.8 %log_probabilities.1 = bf16[4,128,8192]{2,1,0:T(8,128)(2,1)} custom-call(f32[512,8192]{1,0:T(8,128)} %get-tuple-element.5.logits_ref, f32[512,1]{1,0:T(8,128)S(1)} %copy.31.logs_ref, s32[512,1]{1,0:T(8,128)S(1)} %copy-done.5, s32[512,1]{1,0:T(8,128)S(1)} %copy-done.4), custom_call_target="tpu_custom_call" | custom-call | flops 8388608 | bytes 25165824 | tf_op jit(solution)/shard_map/log_probabilities/pallas_call | solution.py:213
  534.9 1.8 fusion.31
  (88 shorter events, 12.6 us)
Async XLA Ops:
  8.0 44.1 %copy-start = (bf16[2048,256]{1,0:T(8,128)(2,1)S(1)}, bf16[2048,256]{1,0:T(8,128)(2,1)}, u32[]{:S(2)}) copy-start(bf16[2048,256]{1,0:T(8,128)(2,1)} %param.26) | copy-start | bytes 3145732
  8.0 124.7 %all-gather.8.cloned.1.call-start = ((), (), s32[]{:S(2)}) async-start(), calls=%async_computation.3 | async-start | bytes 1769472 | tf_op jit(solution)/shard_map/all_gather | solution.py:236
  10.0 2.2 copy-start.2
  12.1 0.9 copy-start.6
  13.1 0.7 copy-start.7
  13.7 4.2 copy-start.15
  17.9 40.8 %copy-start.9 = (bf16[2048]{0:T(1024)(128)(2,1)S(1)}, bf16[2048]{0:T(1024)(128)(2,1)}, u32[]{:S(2)}) copy-start(bf16[2048]{0:T(1024)(128)(2,1)} %param.30) | copy-start | bytes 12292
  17.9 40.8 %copy-start.10 = (bf16[2048]{0:T(1024)(128)(2,1)S(1)}, bf16[2048]{0:T(1024)(128)(2,1)}, u32[]{:S(2)}) copy-start(bf16[2048]{0:T(1024)(128)(2,1)} %param.31) | copy-start | bytes 12292
  17.9 40.9 %copy-start.8 = (bf16[48,2048]{1,0:T(8,128)(2,1)S(1)}, bf16[48,2048]{1,0:T(8,128)(2,1)}, u32[]{:S(2)}) copy-start(bf16[48,2048]{1,0:T(8,128)(2,1)} %param.18) | copy-start | bytes 589828
  53.1 12.4 %all-to-all-start.1 = ((bf16[8,4,256]{2,1,0:T(4,128)(2,1)}), bf16[8,4,256]{2,1,0:T(4,128)(2,1)S(1)}, u32[]{:S(2)}, u32[]{:S(2)}) async-start(bf16[8,4,256]{2,1,0:T(4,128)(2,1)} %all_to_all.22), calls=%async_computation.2 | async-start | bytes 32768 | tf_op jit(solution)/shard_map/all_to_all | solution.py:240
  135.4 11.1 %all-to-all-start = ((bf16[8,48,256]{2,1,0:T(8,128)(2,1)}), bf16[8,48,256]{2,1,0:T(8,128)(2,1)S(1)}, u32[]{:S(2)}, u32[]{:S(2)}) async-start(bf16[8,48,256]{2,1,0:T(8,128)(2,1)} %bitcast.2), calls=%async_computation | async-start | bytes 393216 | tf_op jit(solution)/shard_map/all_to_all | solution.py:240
  138.8 192.2 %all-reduce.3.cloned.1.call-start = ((), (), s32[]{:S(2)}) async-start(), calls=%async_computation.8 | async-start | bytes 2097152
  143.9 262.2 %all-gather.10.cloned.1.call-start = ((), (), s32[]{:S(2)}) async-start(), calls=%async_computation.4 | async-start | bytes 1769472 | tf_op jit(solution)/shard_map/all_gather | solution.py:290
  147.8 0.8 copy-start.11
  147.8 0.8 copy-start.12
  147.9 258.2 %all-gather.12.cloned.1.call-start = ((), (), s32[]{:S(2)}) async-start(), calls=%async_computation.5 | async-start | bytes 15728640 | tf_op jit(solution)/shard_map/all_gather | solution.py:261
  148.6 303.8 %all-gather.14.cloned.1.call-start = ((), (), s32[]{:S(2)}) async-start(), calls=%async_computation.7 | async-start | bytes 2359296 | tf_op jit(solution)/shard_map/all_gather | solution.py:286
  401.3 2.2 copy-start.3
  405.8 128.0 %reduce-scatter.2.cloned.1.call-start = ((), (), s32[]{:S(2)}) async-start(), calls=%async_computation.6 | async-start | bytes 3538944 | tf_op jit(solution)/shard_map/reduce_scatter | solution.py:292
  406.0 5.7 %copy-start.14 = (bf16[384,2048]{1,0:T(8,128)(2,1)S(1)}, bf16[384,2048]{1,0:T(8,128)(2,1)}, u32[]{:S(2)}) copy-start(bf16[384,2048]{1,0:T(8,128)(2,1)} %all-gather.10.cloned.1.call-done) | copy-start | bytes 4718596
  420.9 0.7 copy-start.13
  452.4 68.6 %copy-start.4 = (s32[512,1]{1,0:T(8,128)S(1)}, s32[512,1]{1,0:T(8,128)}, u32[]{:S(2)}) copy-start(s32[512,1]{1,0:T(8,128)} %get-tuple-element.13.end_ref) | copy-start | bytes 6148
  452.4 68.6 %copy-start.5 = (s32[512,1]{1,0:T(8,128)S(1)}, s32[512,1]{1,0:T(8,128)}, u32[]{:S(2)}) copy-start(s32[512,1]{1,0:T(8,128)} %get-tuple-element.14.start_ref) | copy-start | bytes 6148
  521.0 15.8 %copy-start.1 = (bf16[2048,256]{1,0:T(8,128)(2,1)S(1)}, bf16[2048,256]{1,0:T(8,128)(2,1)}, u32[]{:S(2)}) copy-start(bf16[2048,256]{1,0:T(8,128)(2,1)} %param.26) | copy-start | bytes 3145732
Sparse Core Ops, SparseCore 0:
  18.1 47.7 all-gather.7
  148.0 45.5 all-gather.9
  195.2 82.6 all-gather.11
  405.9 46.4 all-gather.13
  456.3 73.1 reduce-scatter.1
Sparse Core Ops, SparseCore 1:
  145.0 185.9 all-reduce.2

commit v2 on v1

--- a/solution.py
+++ b/solution.py
@@ -17,6 +17,8 @@
 SOFTCAP = 30.0
 MIB = 1024 * 1024
 NT = (((1,), (1,)), ((), ()))
+MESH = pl.DeviceIdType.MESH
+PACK = 16 // ACC
 
 
 def rms_scale(values, gain):
@@ -102,34 +104,564 @@
     )(cache_lengths, tree_parents, tree_q, tree_kv[:, 0], tree_kv[:, 1], kv_cache)
 
 
-def draft_kernel(rows_ref, weight_ref, out_ref):
-    width = weight_ref.shape[2]
-    start = pl.multiple_of(lax.axis_index("unit") * width, width)
-    before = jnp.dot(rows_ref[...], weight_ref[0], preferred_element_type=jnp.float32)
-    own = rows_ref[:, pl.ds(start, width)].astype(jnp.float32)
-    out_ref[0] = (own + before * jax.nn.sigmoid(before)).astype(jnp.bfloat16)
-
-
-def draft_columns(rows, draft_weights):
-    count, depth = rows.shape
-    heads, _, width = draft_weights.shape
+def split_unit(size):
+    fast = 2 ** ((size.bit_length() - 1) // 2)
+    return size // fast, fast
+
+
+class Place:
+    def __init__(self):
+        self.reqs, self.units = lax.axis_size("req"), lax.axis_size("unit")
+        self.r, self.u = lax.axis_index("req"), lax.axis_index("unit")
+        self.slow, self.fast = split_unit(self.units)
+        self.z, self.x = self.u // self.fast, lax.rem(self.u, self.fast)
+        self.chips, self.cores = self.reqs // 2, 2
+        self.y, self.c = self.r // 2, lax.rem(self.r, 2)
+
+    def unit(self, dz, dx):
+        return lax.rem(self.z + dz, self.slow) * self.fast + lax.rem(self.x + dx, self.fast)
+
+    def unit_from(self, dz, dx):
+        return self.unit(self.slow - dz, self.fast - dx)
+
+    def req(self, dy, dc):
+        return lax.rem(self.y + dy, self.chips) * 2 + lax.rem(self.c + dc, 2)
+
+    def req_from(self, dy, dc):
+        return self.req(self.chips - dy, 2 - dc)
+
+    def unit_peers(self):
+        return [(dz, dx) for dz in range(self.slow) for dx in range(self.fast) if dz or dx]
+
+    def req_peers(self):
+        return [(dy, dc) for dy in range(self.chips) for dc in range(2) if dy or dc]
+
+
+def meet(at):
+    barrier = pltpu.get_barrier_semaphore()
+    for dz, dx in at.unit_peers():
+        pl.semaphore_signal(
+            barrier, inc=1, device_id=(at.r, at.unit(dz, dx)), device_id_type=MESH
+        )
+    for dy, dc in at.req_peers():
+        pl.semaphore_signal(barrier, inc=1, device_id=(at.req(dy, dc), at.u), device_id_type=MESH)
+    pl.semaphore_wait(barrier, at.units + at.reqs - 2)
+
+
+def push(src, dst, send, recv, r, u):
+    copy = pltpu.make_async_remote_copy(
+        src_ref=src,
+        dst_ref=dst,
+        send_sem=send,
+        recv_sem=recv,
+        device_id=(r, u),
+        device_id_type=MESH,
+    )
+    copy.start()
+    return copy
+
+
+def await_block(at, ref, send, recv):
+    pltpu.make_async_remote_copy(
+        src_ref=ref,
+        dst_ref=ref,
+        send_sem=send,
+        recv_sem=recv,
+        device_id=(at.r, at.u),
+        device_id_type=MESH,
+    ).wait_recv()
+
+
+def gather_units(at, own, buf, send, recv):
+    sent = []
+    for dz in range(1, at.slow):
+        sent.append(
+            push(own, buf.at[at.u], send.at[dz, 0], recv.at[at.u], at.r, at.unit(dz, 0))
+        )
+    for dx in range(1, at.fast):
+        sent.append(
+            push(own, buf.at[at.u], send.at[0, dx], recv.at[at.u], at.r, at.unit(0, dx))
+        )
+    buf[at.u] = own[...]
+    for dz in range(1, at.slow):
+        slot = at.unit_from(dz, 0)
+        await_block(at, buf.at[slot], send.at[dz, 0], recv.at[slot])
+        for dx in range(1, at.fast):
+            sent.append(
+                push(buf.at[slot], buf.at[slot], send.at[dz, dx], recv.at[slot], at.r, at.unit(0, dx))
+            )
+    for dz in range(at.slow):
+        for dx in range(1, at.fast):
+            slot = at.unit_from(dz, dx)
+            await_block(at, buf.at[slot], send.at[dz, dx], recv.at[slot])
+    return sent
+
+
+def layer_kernel(
+    accepted_ref,
+    attended_ref,
+    hidden_ref,
+    out_weight_ref,
+    attn_gain_ref,
+    pre_gain_ref,
+    post_gain_ref,
+    final_gain_ref,
+    mlp_ref,
+    tree_out_ref,
+    path_ref,
+    weights,
+    attended_all,
+    proj_send,
+    proj_recv,
+    first_ref,
+    normed_ref,
+    normed_all,
+    part,
+    sums_send,
+    sums_fast,
+    sums_slow,
+    own_sem,
+    w_send,
+    w_recv,
+    a_send,
+    a_recv,
+    p_send,
+    p_recv,
+    n_send,
+    n_recv,
+    f_send,
+    f_recv,
+    s_send,
+    s_recv,
+):
+    at = Place()
+    units, tree, depth = attended_all.shape
+    matrices = mlp_ref.shape[0]
+    meet(at)
+
+    own_copy = pltpu.make_async_copy(mlp_ref, weights.at[at.r], own_sem)
+    own_copy.start()
+    w_sent = []
+    for m in range(matrices):
+        for dy in range(1, at.chips):
+            w_sent.append(
+                push(
+                    mlp_ref.at[m],
+                    weights.at[at.r, m],
+                    w_send.at[dy, 0, m],
+                    w_recv.at[at.r, m],
+                    at.req(dy, 0),
+                    at.u,
+                )
+            )
+        w_sent.append(
+            push(
+                mlp_ref.at[m],
+                weights.at[at.r, m],
+                w_send.at[0, 1, m],
+                w_recv.at[at.r, m],
+                at.req(0, 1),
+                at.u,
+            )
+        )
+
+    def pass_on(m):
+        for dy in range(1, at.chips):
+            slot = at.req_from(dy, 0)
+            block = weights.at[slot, m]
+            await_block(at, block, w_send.at[dy, 0, m], w_recv.at[slot, m])
+            w_sent.append(
+                push(block, block, w_send.at[dy, 1, m], w_recv.at[slot, m], at.req(0, 1), at.u)
+            )
+
+    sent = gather_units(at, attended_ref, attended_all, a_send, a_recv)
+    columns = jnp.dot(
+        attended_all[...].reshape(units * tree, depth),
+        out_weight_ref[...],
+        preferred_element_type=jnp.float32,
+    ).astype(jnp.bfloat16)
+    proj_send[...] = columns.reshape(proj_send.shape)
+    for dz, dx in at.unit_peers():
+        peer = at.unit(dz, dx)
+        sent.append(
+            push(
+                proj_send.at[peer],
+                proj_recv.at[at.u],
+                p_send.at[dz, dx],
+                p_recv.at[at.u],
+                at.r,
+                peer,
+            )
+        )
+    proj_recv[at.u] = proj_send[at.u]
+    for dz, dx in at.unit_peers():
+        slot = at.unit_from(dz, dx)
+        await_block(at, proj_recv.at[slot], p_send.at[dz, dx], p_recv.at[slot])
+    projected = jnp.concatenate([proj_recv[j] for j in range(units)], axis=1)
+    first = (
+        hidden_ref[...].astype(jnp.float32) + rms_scale(projected, attn_gain_ref[...])
+    ).astype(jnp.bfloat16)
+    first_ref[...] = first
+    normed_ref[...] = rms_scale(first, pre_gain_ref[...]).astype(jnp.bfloat16)
+    pass_on(0)
+    sent += gather_units(at, normed_ref, normed_all, n_send, n_recv)
+    for m in range(1, matrices):
+        pass_on(m)
+
+    own_copy.wait()
+
+    def add_units(slot, start):
+        rows = normed_all[...].reshape(units * tree, depth)
+        gate = jnp.dot(rows, weights[slot, 0], preferred_element_type=jnp.float32)
+        upward = jnp.dot(rows, weights[slot, 1], preferred_element_type=jnp.float32)
+        active = (jax.nn.gelu(gate, approximate=True) * upward).astype(jnp.bfloat16)
+        terms = dot_nt(active, weights[slot, 2]).reshape(units, tree, depth)
+        part[...] = terms if start else part[...] + terms
+
+    add_units(at.r, True)
+
+    def one_chip(dy, carry):
+        @pl.when(dy > 0)
+        def _():
+            add_units(at.req_from(dy, 0), False)
+
+        slot = at.req_from(dy, 1)
+        for m in range(matrices):
+            await_block(at, weights.at[slot, m], w_send.at[0, 1, m], w_recv.at[slot, m])
+        add_units(slot, False)
+        return carry
+
+    lax.fori_loop(0, at.chips, one_chip, 0)
+
+    order = list(range(1, at.slow)) + [0]
+    for dz in order:
+        for dx in range(1, at.fast):
+            peer = at.unit(dz, dx)
+            zt = peer // at.fast
+            sums_send[peer] = part[peer].astype(jnp.bfloat16)
+            sent.append(
+                push(
+                    sums_send.at[peer],
+                    sums_fast.at[zt, at.x],
+                    f_send.at[dz, dx],
+                    f_recv.at[zt, at.x],
+                    at.r,
+                    at.unit(0, dx),
+                )
+            )
+    for dz in order:
+        target = at.unit(dz, 0)
+        zt = target // at.fast
+        total = part[target]
+        for dx in range(1, at.fast):
+            xs = lax.rem(at.x + at.fast - dx, at.fast)
+            await_block(at, sums_fast.at[zt, xs], f_send.at[dz, dx], f_recv.at[zt, xs])
+            total = total + sums_fast[zt, xs].astype(jnp.float32)
+        if dz:
+            sums_send[target] = total.astype(jnp.bfloat16)
+            sent.append(
+                push(
+                    sums_send.at[target],
+                    sums_slow.at[at.z],
+                    s_send.at[dz],
+                    s_recv.at[at.z],
+                    at.r,
+                    target,
+                )
+            )
+    for dz in range(1, at.slow):
+        zs = lax.rem(at.z + at.slow - dz, at.slow)
+        await_block(at, sums_slow.at[zs], s_send.at[dz], s_recv.at[zs])
+        total = total + sums_slow[zs].astype(jnp.float32)
+    tree_out = (
+        first_ref[...].astype(jnp.float32) + rms_scale(total, post_gain_ref[...])
+    ).astype(jnp.bfloat16)
+    tree_out_ref[...] = tree_out
+
+    ready = rms_scale(tree_out, final_gain_ref[...]).astype(jnp.bfloat16)
+    width = depth // PACK
+    row = lax.broadcasted_iota(jnp.int32, (PACK * ACC, tree), 0)
+    node = lax.broadcasted_iota(jnp.int32, (PACK * ACC, tree), 1)
+    packed = jnp.zeros((PACK * ACC, width), jnp.float32)
+    for chunk in range(PACK):
+        pick = jnp.zeros((PACK * ACC, tree), jnp.float32)
+        for i in range(ACC):
+            hit = (row == chunk * ACC + i) & (node == accepted_ref[0, i])
+            pick = jnp.where(hit, 1.0, pick)
+        packed = packed + jnp.dot(
+            pick.astype(jnp.bfloat16),
+            ready[:, chunk * width : (chunk + 1) * width],
+            preferred_element_type=jnp.float32,
+        )
+    path_ref[...] = packed.astype(jnp.bfloat16)
+    for copy in sent + w_sent:
+        copy.wait_send()
+
+
+def layer(attended, hidden, accepted, out_weight, mlp_weights, gains):
+    reqs, units = lax.axis_size("req"), lax.axis_size("unit")
+    slow, fast = split_unit(units)
+    tree, depth = hidden.shape
+    bf16, dma = jnp.bfloat16, pltpu.SemaphoreType.DMA
+    vmem = pl.BlockSpec(memory_space=pltpu.VMEM)
+    rows = (units, tree, depth)
+    cols = (units, tree, out_weight.shape[1])
+    matrices, _, width = mlp_weights.shape
     return pl.pallas_call(
-        draft_kernel,
-        grid=(heads,),
-        out_shape=jax.ShapeDtypeStruct((heads, count, width), jnp.bfloat16),
-        in_specs=[
-            pl.BlockSpec((count, depth), lambda h: (0, 0)),
-            pl.BlockSpec((1, depth, width), lambda h: (h, 0, 0)),
+        layer_kernel,
+        out_shape=(
+            jax.ShapeDtypeStruct((tree, depth), bf16),
+            jax.ShapeDtypeStruct((PACK * ACC, depth // PACK), bf16),
+        ),
+        in_specs=[pl.BlockSpec(memory_space=pltpu.SMEM)]
+        + [vmem] * 7
+        + [pl.BlockSpec(memory_space=pl.ANY)],
+        out_specs=(vmem, vmem),
+        scratch_shapes=[
+            pltpu.VMEM((reqs, matrices, depth, width), bf16),
+            pltpu.VMEM(rows, bf16),
+            pltpu.VMEM(cols, bf16),
+            pltpu.VMEM(cols, bf16),
+            pltpu.VMEM((tree, depth), bf16),
+            pltpu.VMEM((tree, depth), bf16),
+            pltpu.VMEM(rows, bf16),
+            pltpu.VMEM(rows, jnp.float32),
+            pltpu.VMEM(rows, bf16),
+            pltpu.VMEM((slow, fast, tree, depth), bf16),
+            pltpu.VMEM((slow, tree, depth), bf16),
+            dma(()),
+            dma((reqs // 2, 2, matrices)),
+            dma((reqs, matrices)),
+            dma((slow, fast)),
+            dma((units,)),
+            dma((slow, fast)),
+            dma((units,)),
+            dma((slow, fast)),
+            dma((units,)),
+            dma((slow, fast)),
+            dma((slow, fast)),
+            dma((slow,)),
+            dma((slow,)),
         ],
-        out_specs=pl.BlockSpec((1, count, width), lambda h: (h, 0, 0)),
-        compiler_params=pltpu.CompilerParams(vmem_limit_bytes=24 * MIB),
-        cost_estimate=pl.CostEstimate(
-            flops=2 * heads * count * depth * width,
-            bytes_accessed=2 * heads * depth * width,
-            transcendentals=heads * count * width,
+        compiler_params=pltpu.CompilerParams(
+            collective_id=0, has_side_effects=True, vmem_limit_bytes=56 * MIB
+        ),
+        name="projection_and_feed_forward",
+    )(accepted, attended, hidden, out_weight, *[g[None, :] for g in gains], mlp_weights)
+
+
+def drafts_kernel(
+    path_ref,
+    weight_ref,
+    out_ref,
+    paths,
+    every,
+    weight,
+    drafts,
+    own_sem,
+    l_send,
+    l_recv,
+    m_send,
+    m_recv,
+    a_send,
+    a_recv,
+    q_send,
+    q_recv,
+):
+    at = Place()
+    reqs, units, packed, wide = paths.shape
+    heads = weight_ref.shape[0]
+    rows, depth = every.shape
+    share, width = drafts.shape[2:]
+    head = at.r * heads // reqs
+    load = pltpu.make_async_copy(weight_ref.at[head], weight, own_sem)
+    load.start()
+    meet(at)
+
+    sent = []
+    for dz, dx in at.unit_peers():
+        sent.append(
+            push(
+                path_ref,
+                paths.at[at.r, at.u],
+                l_send.at[dz, dx],
+                l_recv.at[at.u],
+                at.r,
+                at.unit(dz, dx),
+            )
+        )
+    paths[at.r, at.u] = path_ref[...]
+    for dz, dx in at.unit_peers():
+        slot = at.unit_from(dz, dx)
+        await_block(at, paths.at[at.r, slot], l_send.at[dz, dx], l_recv.at[slot])
+    for dy, dc in at.req_peers():
+        sent.append(
+            push(
+                paths.at[at.r],
+                paths.at[at.r],
+                m_send.at[dy, dc],
+                m_recv.at[at.r],
+                at.req(dy, dc),
+                at.u,
+            )
+        )
+    for dy, dc in at.req_peers():
+        slot = at.req_from(dy, dc)
+        await_block(at, paths.at[slot], m_send.at[dy, dc], m_recv.at[slot])
+    flat = paths[...].reshape(reqs * units * packed, wide)
+    row = lax.broadcasted_iota(jnp.int32, (rows, flat.shape[0]), 0)
+    place = lax.broadcasted_iota(jnp.int32, (rows, flat.shape[0]), 1)
+    base = row // ACC * packed + lax.rem(row, ACC)
+    for chunk in range(PACK):
+        pick = jnp.where(place == base + chunk * ACC, 1.0, 0.0).astype(jnp.bfloat16)
+        every[:, chunk * wide : (chunk + 1) * wide] = jnp.dot(
+            pick, flat, preferred_element_type=jnp.float32
+        ).astype(jnp.bfloat16)
+
+    load.wait()
+    if share == rows:
+        mine = every.at[:, :]
+    else:
+        start = pl.multiple_of(lax.rem(at.r * share, rows), share)
+        mine = every.at[pl.ds(start, share), :]
+    before = jnp.dot(mine[...], weight[...], preferred_element_type=jnp.float32)
+    own = mine[:, pl.ds(pl.multiple_of(at.u * width, width), width)].astype(jnp.float32)
+    drafts[at.r, at.u] = (own + before * jax.nn.sigmoid(before)).astype(jnp.bfloat16)
+
+    block = drafts.at[at.r, at.u]
+    for dz in range(1, at.slow):
+        sent.append(push(block, block, a_send.at[dz, 0], a_recv.at[at.u], at.r, at.unit(dz, 0)))
+    for dz in range(at.slow):
+        slot = at.unit_from(dz, 0)
+        block = drafts.at[at.r, slot]
+        if dz:
+            await_block(at, block, a_send.at[dz, 0], a_recv.at[slot])
+        for dx in range(1, at.fast):
+            sent.append(push(block, block, a_send.at[dz, dx], a_recv.at[slot], at.r, at.unit(0, dx)))
+    for dz in range(at.slow):
+        for dx in range(1, at.fast):
+            slot = at.unit_from(dz, dx)
+            await_block(at, drafts.at[at.r, slot], a_send.at[dz, dx], a_recv.at[slot])
+    block = drafts.at[at.r]
+    for dy in range(1, at.chips):
+        sent.append(push(block, block, q_send.at[dy, 0], q_recv.at[at.r], at.req(dy, 0), at.u))
+    for dy in range(at.chips):
+        slot = at.req_from(dy, 0)
+        block = drafts.at[slot]
+        if dy:
+            await_block(at, block, q_send.at[dy, 0], q_recv.at[slot])
+        sent.append(push(block, block, q_send.at[dy, 1], q_recv.at[slot], at.req(0, 1), at.u))
+    for dy in range(at.chips):
+        slot = at.req_from(dy, 1)
+        await_block(at, drafts.at[slot], q_send.at[dy, 1], q_recv.at[slot])
+    for k in range(reqs):
+        for j in range(units):
+            out_ref[k * share : (k + 1) * share, j * width : (j + 1) * width] = drafts[k, j]
+    for copy in sent:
+        copy.wait_send()
+
+
+def gather_drafts(path, draft_weights):
+    reqs, units = lax.axis_size("req"), lax.axis_size("unit")
+    slow, fast = split_unit(units)
+    heads, depth, width = draft_weights.shape
+    rows = reqs * units * ACC
+    share = heads * rows // reqs
+    bf16, dma = jnp.bfloat16, pltpu.SemaphoreType.DMA
+    vmem = pl.BlockSpec(memory_space=pltpu.VMEM)
+    return pl.pallas_call(
+        drafts_kernel,
+        out_shape=jax.ShapeDtypeStruct((heads * rows, depth), bf16),
+        in_specs=[vmem, pl.BlockSpec(memory_space=pl.ANY)],
+        out_specs=vmem,
+        scratch_shapes=[
+            pltpu.VMEM((reqs, units) + path.shape, bf16),
+            pltpu.VMEM((rows, depth), bf16),
+            pltpu.VMEM((depth, width), bf16),
+            pltpu.VMEM((reqs, units, share, width), bf16),
+            dma(()),
+            dma((slow, fast)),
+            dma((units,)),
+            dma((reqs // 2, 2)),
+            dma((reqs,)),
+            dma((slow, fast)),
+            dma((units,)),
+            dma((reqs // 2, 2)),
+            dma((reqs,)),
+        ],
+        compiler_params=pltpu.CompilerParams(
+            collective_id=1, has_side_effects=True, vmem_limit_bytes=48 * MIB
         ),
         name="draft_heads",
-    )(rows, draft_weights)
+    )(path, draft_weights)
+
+
+def sum_kernel(own_ref, out_ref, unit_parts, group, req_parts, u_send, u_recv, r_send, r_recv):
+    at = Place()
+    meet(at)
+    sent = []
+    for dz, dx in at.unit_peers():
+        sent.append(
+            push(
+                own_ref,
+                unit_parts.at[at.u],
+                u_send.at[dz, dx],
+                u_recv.at[at.u],
+                at.r,
+                at.unit(dz, dx),
+            )
+        )
+    unit_parts[at.u] = own_ref[...]
+    for dz, dx in at.unit_peers():
+        slot = at.unit_from(dz, dx)
+        await_block(at, unit_parts.at[slot], u_send.at[dz, dx], u_recv.at[slot])
+    group[...] = jnp.sum(unit_parts[...], axis=0)
+    for dy, dc in at.req_peers():
+        sent.append(
+            push(
+                group,
+                req_parts.at[at.r],
+                r_send.at[dy, dc],
+                r_recv.at[at.r],
+                at.req(dy, dc),
+                at.u,
+            )
+        )
+    req_parts[at.r] = group[...]
+    for dy, dc in at.req_peers():
+        slot = at.req_from(dy, dc)
+        await_block(at, req_parts.at[slot], r_send.at[dy, dc], r_recv.at[slot])
+    out_ref[...] = jnp.sum(req_parts[...], axis=0)
+    for copy in sent:
+        copy.wait_send()
+
+
+def sum_over_devices(values):
+    reqs, units = lax.axis_size("req"), lax.axis_size("unit")
+    slow, fast = split_unit(units)
+    lines = max(8, values.shape[0] // 128)
+    block = (lines, 128)
+    f32, dma = jnp.float32, pltpu.SemaphoreType.DMA
+    vmem = pl.BlockSpec(memory_space=pltpu.VMEM)
+    padded = jnp.pad(values, (0, lines * 128 - values.shape[0])).reshape(block)
+    summed = pl.pallas_call(
+        sum_kernel,
+        out_shape=jax.ShapeDtypeStruct(block, f32),
+        in_specs=[vmem],
+        out_specs=vmem,
+        scratch_shapes=[
+            pltpu.VMEM((units,) + block, f32),
+            pltpu.VMEM(block, f32),
+            pltpu.VMEM((reqs,) + block, f32),
+            dma((slow, fast)),
+            dma((units,)),
+            dma((reqs // 2, 2)),
+            dma((reqs,)),
+        ],
+        compiler_params=pltpu.CompilerParams(collective_id=2, has_side_effects=True),
+        name="sum_of_totals",
+    )(padded)
+    return summed.reshape(-1)[: values.shape[0]]
 
 
 def allowed_ids(start, end, first_id, shape):
@@ -137,23 +669,21 @@
     return (ids >= start) & (ids < end)
 
 
-def logits_kernel(chunk, drafts_ref, emb_ref, start_ref, end_ref, logits_ref, sums_ref, rows_ref):
+def logits_kernel(chunk, drafts_ref, emb_ref, start_ref, end_ref, logits_ref, sums_ref):
     step = pl.program_id(0)
-    blocks, count, width = drafts_ref.shape
+    count = drafts_ref.shape[0]
     tile = emb_ref.shape[0]
     vocab = tile * pl.num_programs(0)
     first_id = (lax.axis_index("req") * lax.axis_size("unit") + lax.axis_index("unit")) * vocab
 
     @pl.when(step == 0)
     def _():
-        for b in range(blocks):
-            rows_ref[:, b * width : (b + 1) * width] = drafts_ref[b]
         sums_ref[...] = jnp.zeros_like(sums_ref)
 
     start, end = start_ref[...], end_ref[...]
     for c in range(tile // chunk):
         span = slice(c * chunk, (c + 1) * chunk)
-        products = dot_nt(rows_ref[...], emb_ref[span, :])
+        products = dot_nt(drafts_ref[...], emb_ref[span, :])
         logits = SOFTCAP * jnp.tanh(products * (1.0 / SOFTCAP))
         logits_ref[:, span] = logits
         keep = allowed_ids(start, end, first_id + step * tile + c * chunk, logits.shape)
@@ -176,7 +706,7 @@
 
 
 def vocabulary(drafts, embedding, tenant_ranges):
-    blocks, count, width = drafts.shape
+    count = drafts.shape[0]
     vocab, depth = embedding.shape
     rows = count // HEADS
     bounds = jnp.tile(jnp.repeat(tenant_ranges, ACC, axis=0), (HEADS, 1))
@@ -191,7 +721,7 @@
             jax.ShapeDtypeStruct((count, 128), jnp.float32),
         ),
         in_specs=[
-            pl.BlockSpec((blocks, count, width), lambda i: (0, 0, 0)),
+            pl.BlockSpec((count, depth), lambda i: (0, 0)),
             pl.BlockSpec((tile, depth), lambda i: (i, 0)),
             once,
             once,
@@ -200,7 +730,6 @@
             pl.BlockSpec((count, tile), lambda i: (0, i)),
             pl.BlockSpec((count, 128), lambda i: (0, 0)),
         ),
-        scratch_shapes=[pltpu.VMEM((count, depth), jnp.bfloat16)],
         compiler_params=pltpu.CompilerParams(vmem_limit_bytes=56 * MIB),
         cost_estimate=pl.CostEstimate(
             flops=2 * count * depth * vocab,
@@ -209,7 +738,7 @@
         ),
         name="vocabulary_logits",
     )(drafts, embedding, starts, ends)
-    totals = lax.psum(jnp.sum(sums, axis=1), ("req", "unit"))
+    totals = sum_over_devices(jnp.sum(sums, axis=1))
     return pl.pallas_call(
         finish_kernel,
         grid=(vocab // tile,),
@@ -222,22 +751,6 @@
         ),
         name="log_probabilities",
     )(logits, jnp.log(totals)[:, None], starts, ends)
-
-
-def unit_terms(mlp_rows, weight_part):
-    gate_part = jnp.dot(mlp_rows, weight_part[0], preferred_element_type=jnp.float32)
-    upward = jnp.dot(mlp_rows, weight_part[1], preferred_element_type=jnp.float32)
-    active = (jax.nn.gelu(gate_part, approximate=True) * upward).astype(jnp.bfloat16)
-    return dot_nt(active, weight_part[2])
-
-
-def project_rows(attended, out_weight):
-    cols = jnp.dot(
-        lax.all_gather(attended, "unit", axis=0, tiled=True),
-        out_weight,
-        preferred_element_type=jnp.float32,
-    ).astype(jnp.bfloat16)
-    return lax.all_to_all(cols, "unit", split_axis=0, concat_axis=1, tiled=True)
 
 
 def per_device(
@@ -258,39 +771,11 @@
     ff_post_gain,
     final_gain,
 ):
-    group_weights = lax.all_gather(mlp_weights, "req", axis=2, tiled=True)
     attended = attend(tree_q, tree_kv, kv_cache, cache_lengths, tree_parents)
-
-    def after_attention(residual, projected):
-        first = (residual.astype(jnp.float32) + rms_scale(projected, attn_post_gain)).astype(
-            jnp.bfloat16
-        )
-        return first, rms_scale(first, ff_pre_gain).astype(jnp.bfloat16)
-
-    def after_mlp(first, mlp_sum):
-        return (first.astype(jnp.float32) + rms_scale(mlp_sum, ff_post_gain)).astype(jnp.bfloat16)
-
-    path_attended = jnp.take(attended, accepted[0], axis=0)
-    path_hidden = jnp.take(hidden, accepted[0], axis=0)
-    path_first, path_mlp_rows = after_attention(
-        path_hidden, project_rows(path_attended, out_weight)
-    )
-    partial = unit_terms(
-        lax.all_gather(path_mlp_rows, ("req", "unit"), axis=0, tiled=True), mlp_weights
-    )
-    path_sum = lax.psum_scatter(partial, ("req", "unit"), scatter_dimension=0, tiled=True)
-    path_normed = rms_scale(after_mlp(path_first, path_sum), final_gain).astype(jnp.bfloat16)
-    every_row = lax.all_gather(path_normed, ("req", "unit"), axis=0, tiled=True)
-    own = draft_columns(every_row, draft_weights)
-    own = own.reshape(own.shape[0] * own.shape[1], own.shape[2])
-    drafts = lax.all_gather(own, "unit", axis=0)
-    draft_logprobs = vocabulary(drafts, embedding, tenant_ranges)
-
-    first, normed = after_attention(hidden, project_rows(attended, out_weight))
-    mlp_rows = lax.all_gather(normed, "unit", axis=0, tiled=True)
-    partial_sums = unit_terms(mlp_rows, group_weights)
-    mlp_sum = lax.psum_scatter(partial_sums, "unit", scatter_dimension=0, tiled=True)
-    return (after_mlp(first, mlp_sum), draft_logprobs)
+    gains = (attn_post_gain, ff_pre_gain, ff_post_gain, final_gain)
+    tree_out, path = layer(attended, hidden, accepted, out_weight, mlp_weights, gains)
+    drafts = gather_drafts(path, draft_weights)
+    return (tree_out, vocabulary(drafts, embedding, tenant_ranges))
 
 
 def solution(mesh):

time: 545 us -> 222 us (0.41)
  waiting for transfers between devices: 222 us -> 0 us
  blocking collectives: 207 us -> 0 us
  Pallas kernels: 46.9 us -> 202 us
  matrix products: 22.8 us -> 0 us
  between operations: 16.3 us -> 1.4 us
  starting transfers between devices: 9.5 us -> 0 us
  other arithmetic: 7.96 us -> 1.09 us
    unnamed x7 -> x0, waiting for transfers between devices: 183 us -> none
    all_gather x3 -> x0, blocking collectives: 167 us -> none  [the longest x1 68.1 us: per_device(): every_row = lax.all_gather(path_normed, ('req', 'unit'), axis=0, tiled=True)]
    pallas_call x1 -> x3, Pallas kernels: 2.24 us -> 158 us  [the longest x1 107 us: layer(): pl.pallas_call(layer_kernel, out_shape=(jax.ShapeDtypeStruct((tree, depth...]
    psum x1 -> x0, blocking collectives: 39.6 us -> none  [vocabulary(): totals = lax.psum(jnp.sum(sums, axis=1), ('req', 'unit'))]
    all_gather x4 -> x0, waiting for transfers between devices: 29.8 us -> none  [the longest x1 29.8 us: per_device(): drafts = lax.all_gather(own, 'unit', axis=0)]
    dot_general x6 -> x0, matrix products: 22.8 us -> none  [the longest x2 12.6 us: dot_nt(): return lax.dot_general(left, right, NT, preferred_element_type=jnp.float32)]
    all_to_all x2 -> x0, starting transfers between devices: 9.08 us -> none  [project_rows(): return lax.all_to_all(cols, 'unit', split_axis=0, concat_axis=1, tiled=True)]
    all_to_all x2 -> x0, waiting for transfers between devices: 8.74 us -> none  [project_rows(): return lax.all_to_all(cols, 'unit', split_axis=0, concat_axis=1, tiled=True)]
  transfers between devices with their start and end apart: 8 -> 0, of which waited for: 4 -> 0; matrix products, arithmetic and copies ran while one was open for 5% -> 0% of each run, Pallas kernels for 8% -> 0%
where the time goes in v2:
time: 222 us; the launch traced here: 221 us
  Pallas kernels  202 us (91%)
  local copies, waits for them, and re-layouts  16.5 us (7%)
    pallas_call x1, Pallas kernels, layer(): pl.pallas_call(layer_kernel, out_shape=(jax.ShapeDtypeStruct((tree, depth...  107 us
    pallas_call x1, Pallas kernels, gather_drafts(): pl.pallas_call(drafts_kernel, out_shape=jax.ShapeDtypeStruct((heads * row...  41.6 us
    pallas_call x1, Pallas kernels, vocabulary(): pl.pallas_call(functools.partial(logits_kernel, min(256, tile)), grid=(vo...  27.4 us
    pallas_call x1, Pallas kernels, vocabulary(): pl.pallas_call(finish_kernel, grid=(vocab // tile,), out_shape=jax.ShapeD...  12.7 us
    pallas_call x1, Pallas kernels, sum_over_devices(): pl.pallas_call(sum_kernel, out_shape=jax.ShapeDtypeStruct(block, f32), in...  10.1 us
    unnamed x20, local copies, waits for them, and re-layouts  7.91 us
    broadcast_in_dim x4, local copies, waits for them, and re-layouts, layer(): g[None, :]  5.13 us

profile of v2, /device:TPU:0, one launch (start us, length us, event | category | flops | bytes accessed | tf_op | source)
XLA Modules:
  0.0 221.0 jit_solution(10694643335606941032)
XLA Ops:
  1.3 1.3 broadcast_in_dim.16.attn_gain_ref
  2.6 1.3 broadcast_in_dim.17.pre_gain_ref
  3.9 1.3 broadcast_in_dim.18.post_gain_ref
  5.1 1.3 broadcast_in_dim.19.final_gain_ref
  6.4 0.8 copy.23
  7.2 1.1 fusion.1
  8.4 2.2 copy-done
  10.6 0.9 copy-done.5
  11.5 0.7 copy-done.7
  12.2 3.6 %tree_attention.1.attended_ref = bf16[48,2048]{1,0:T(8,128)(2,1)S(1)} custom-call(s32[1]{0:T(128)S(6)} %copy.30.length_ref, s32[1,48]{1,0:T(1,128)S(1)} %copy-done.7, bf16[48,2048]{1,0:T(8,128)(2,1)S(1)} %copy-done.5, bf16[48,512]{1,0:T(8,128)(2,1)S(1)} %get-tuple-element.15.tk_ref, bf16[48,512]{1,0:T(8,128)(2,1)S(1)} %get-tuple-element.14.tv_ref, ...), custom_call_target="tpu_custom_call" | custom-call | flops 805306368 | bytes 8388608 | tf_op jit(solution)/shard_map/tree_attention/pallas_call | solution.py:84
  15.8 0.7 copy-done.4
  16.4 106.7 %projection_and_feed_forward.1 = (bf16[48,2048]{1,0:T(8,128)(2,1)}, bf16[16,512]{1,0:T(8,128)(2,1)}) custom-call(s32[1,4]{1,0:T(1,128)} %accepted_ref.1, bf16[48,2048]{1,0:T(8,128)(2,1)} %copy-done.4, bf16[48,2048]{1,0:T(8,128)(2,1)} %hidden_ref.1, bf16[2048,256]{1,0:T(8,128)(2,1)} %out_weight_ref.1, bf16[1,2048]{1,0:T(2,128)(2,1)} %broadcast_in_dim.16.attn_gain_ref, ...), custom_call_target="tpu_custom_call" | custom-call | tf_op jit(solution)/shard_map/projection_and_feed_forward/pallas_call | solution.py:410
  123.1 0.9 fusion
  124.0 0.7 copy-done.6
  124.7 41.6 %draft_heads.1.drafts_ref = bf16[512,2048]{1,0:T(8,128)(2,1)S(1)} custom-call(bf16[16,512]{1,0:T(8,128)(2,1)S(1)} %copy-done.6, bf16[4,2048,256]{2,1,0:T(8,128)(2,1)} %weight_ref.1), custom_call_target="tpu_custom_call" | custom-call | tf_op jit(solution)/shard_map/draft_heads/pallas_call | solution.py:572
  166.3 1.3 copy-done.1
  167.6 27.4 %vocabulary_logits.1 = (f32[512,8192]{1,0:T(8,128)}, f32[512,128]{1,0:T(8,128)}) custom-call(bf16[512,2048]{1,0:T(8,128)(2,1)} %copy-done.1, bf16[8192,2048]{1,0:T(8,128)(2,1)} %emb_ref.1, s32[512,1]{1,0:T(8,128)} %get-tuple-element.11.start_ref, s32[512,1]{1,0:T(8,128)} %get-tuple-element.10.end_ref), custom_call_target="tpu_custom_call" | custom-call | flops 17179869184 | bytes 50331648 | tf_op jit(solution)/shard_map/vocabulary_logits/pallas_call | solution.py:716
  195.0 1.1 reduce_sum.9
  196.1 0.6 pad_bitcast_fusion.own_ref
  196.7 10.1 %sum_of_totals.1 = f32[8,128]{1,0:T(8,128)} custom-call(f32[8,128]{1,0:T(8,128)} %pad_bitcast_fusion.own_ref), custom_call_target="tpu_custom_call" | custom-call | tf_op jit(solution)/shard_map/sum_of_totals/pallas_call | solution.py:647
  206.8 0.7 slice_log_fusion
  207.4 0.2 copy.24.logs_ref
  207.6 12.7 %log_probabilities.1 = bf16[4,128,8192]{2,1,0:T(8,128)(2,1)} custom-call(f32[512,8192]{1,0:T(8,128)} %get-tuple-element.8.logits_ref, f32[512,1]{1,0:T(8,128)S(1)} %copy.24.logs_ref, s32[512,1]{1,0:T(8,128)S(1)} %copy-done.3, s32[512,1]{1,0:T(8,128)S(1)} %copy-done.2), custom_call_target="tpu_custom_call" | custom-call | flops 8388608 | bytes 25165824 | tf_op jit(solution)/shard_map/log_probabilities/pallas_call | solution.py:742
  220.3 0.7 copy.31
  (15 shorter events, 0.1 us)
Async XLA Ops:
  8.4 2.2 copy-start
  10.6 0.9 copy-start.5
  11.5 0.7 copy-start.7
  15.7 0.7 copy-start.4
  124.0 0.7 copy-start.6
  166.3 1.3 copy-start.1
  167.6 40.0 %copy-start.2 = (s32[512,1]{1,0:T(8,128)S(1)}, s32[512,1]{1,0:T(8,128)}, u32[]{:S(2)}) copy-start(s32[512,1]{1,0:T(8,128)} %get-tuple-element.10.end_ref) | copy-start | bytes 6148
  167.6 40.0 %copy-start.3 = (s32[512,1]{1,0:T(8,128)S(1)}, s32[512,1]{1,0:T(8,128)}, u32[]{:S(2)}) copy-start(s32[512,1]{1,0:T(8,128)} %get-tuple-element.11.start_ref) | copy-start | bytes 6148
  207.6 12.7 %copy-start.8 = (bf16[48,2048]{1,0:T(8,128)(2,1)S(1)}, bf16[48,2048]{1,0:T(8,128)(2,1)}, u32[]{:S(2)}) copy-start(bf16[48,2048]{1,0:T(8,128)(2,1)} %get-tuple-element.18) | copy-start | bytes 589828

commit v3 on v2

--- a/solution.py
+++ b/solution.py
@@ -172,7 +172,7 @@
     ).wait_recv()
 
 
-def gather_units(at, own, buf, send, recv):
+def start_gather(at, own, buf, send, recv):
     sent = []
     for dz in range(1, at.slow):
         sent.append(
@@ -183,6 +183,11 @@
             push(own, buf.at[at.u], send.at[0, dx], recv.at[at.u], at.r, at.unit(0, dx))
         )
     buf[at.u] = own[...]
+    return sent
+
+
+def forward_gather(at, buf, send, recv):
+    sent = []
     for dz in range(1, at.slow):
         slot = at.unit_from(dz, 0)
         await_block(at, buf.at[slot], send.at[dz, 0], recv.at[slot])
@@ -190,11 +195,99 @@
             sent.append(
                 push(buf.at[slot], buf.at[slot], send.at[dz, dx], recv.at[slot], at.r, at.unit(0, dx))
             )
+    return sent
+
+
+def end_gather(at, buf, send, recv):
     for dz in range(at.slow):
         for dx in range(1, at.fast):
             slot = at.unit_from(dz, dx)
             await_block(at, buf.at[slot], send.at[dz, dx], recv.at[slot])
+
+
+def start_packed(at, own, buf, send, recv):
+    sent = []
+    for dz, dx in at.unit_peers():
+        sent.append(
+            push(own, buf.at[at.r, at.u], send.at[dz, dx], recv.at[at.u], at.r, at.unit(dz, dx))
+        )
+    buf[at.r, at.u] = own[...]
     return sent
+
+
+def spread_packed(at, buf, l_send, l_recv, m_send, m_recv):
+    sent = []
+    for dz, dx in at.unit_peers():
+        slot = at.unit_from(dz, dx)
+        await_block(at, buf.at[at.r, slot], l_send.at[dz, dx], l_recv.at[slot])
+    block = buf.at[at.r]
+    for dy, dc in at.req_peers():
+        sent.append(
+            push(block, block, m_send.at[dy, dc], m_recv.at[at.r], at.req(dy, dc), at.u)
+        )
+    return sent
+
+
+def end_packed(at, buf, send, recv):
+    for dy, dc in at.req_peers():
+        slot = at.req_from(dy, dc)
+        await_block(at, buf.at[slot], send.at[dy, dc], recv.at[slot])
+
+
+def pack_rows(accepted_ref, values):
+    tree, depth = values.shape
+    width = depth // PACK
+    row = lax.broadcasted_iota(jnp.int32, (PACK * ACC, tree), 0)
+    node = lax.broadcasted_iota(jnp.int32, (PACK * ACC, tree), 1)
+    packed = jnp.zeros((PACK * ACC, width), jnp.float32)
+    for chunk in range(PACK):
+        pick = jnp.zeros((PACK * ACC, tree), jnp.float32)
+        for i in range(ACC):
+            hit = (row == chunk * ACC + i) & (node == accepted_ref[0, i])
+            pick = jnp.where(hit, 1.0, pick)
+        packed = packed + jnp.dot(
+            pick.astype(jnp.bfloat16),
+            values[:, chunk * width : (chunk + 1) * width],
+            preferred_element_type=jnp.float32,
+        )
+    return packed
+
+
+def packed_places(rows, chunk):
+    shape = (rows, rows * PACK)
+    row = lax.broadcasted_iota(jnp.int32, shape, 0)
+    place = lax.broadcasted_iota(jnp.int32, shape, 1)
+    base = row // ACC * (PACK * ACC) + lax.rem(row, ACC)
+    return jnp.where(place == base + chunk * ACC, 1.0, 0.0).astype(jnp.bfloat16)
+
+
+def unpack_rows(buf, every):
+    reqs, units, packed, wide = buf.shape
+    rows = units * ACC
+    for k in range(reqs):
+        flat = buf[k].reshape(units * packed, wide)
+        for chunk in range(PACK):
+            every[k * rows : (k + 1) * rows, chunk * wide : (chunk + 1) * wide] = jnp.dot(
+                packed_places(rows, chunk), flat, preferred_element_type=jnp.float32
+            ).astype(jnp.bfloat16)
+
+
+def packed_rms(values, gain):
+    width = values.shape[1]
+    squares = jnp.sum(values * values, axis=1, keepdims=True)
+    total = squares[:ACC]
+    for chunk in range(1, PACK):
+        total = total + squares[chunk * ACC : (chunk + 1) * ACC]
+    factor = lax.rsqrt(total / (PACK * width) + EPS)
+    gains = [
+        jnp.broadcast_to(gain[:, chunk * width : (chunk + 1) * width], (ACC, width))
+        for chunk in range(PACK)
+    ]
+    return (
+        values
+        * jnp.concatenate([factor] * PACK, axis=0)
+        * jnp.concatenate(gains, axis=0).astype(jnp.float32)
+    )
 
 
 def layer_kernel(
@@ -202,13 +295,11 @@
     attended_ref,
     hidden_ref,
     out_weight_ref,
-    attn_gain_ref,
-    pre_gain_ref,
-    post_gain_ref,
-    final_gain_ref,
+    gains_ref,
     mlp_ref,
+    draft_ref,
     tree_out_ref,
-    path_ref,
+    drafts_ref,
     weights,
     attended_all,
     proj_send,
@@ -217,7 +308,6 @@
     normed_ref,
     normed_all,
     part,
-    sums_send,
     sums_fast,
     sums_slow,
     own_sem,
@@ -233,16 +323,54 @@
     f_recv,
     s_send,
     s_recv,
+    pack_one,
+    paths_one,
+    pack_two,
+    paths_two,
+    every,
+    path_part,
+    path_req,
+    path_units,
+    path_in,
+    draft_weight,
+    drafts,
+    draft_sem,
+    l1_send,
+    l1_recv,
+    m1_send,
+    m1_recv,
+    l2_send,
+    l2_recv,
+    m2_send,
+    m2_recv,
+    e_send,
+    e_recv,
+    g_send,
+    g_recv,
+    h_send,
+    h_recv,
+    q_send,
+    q_recv,
+    out_sem,
 ):
     at = Place()
     units, tree, depth = attended_all.shape
     matrices = mlp_ref.shape[0]
+    reqs = at.reqs
+    heads = draft_ref.shape[0]
+    attn_gain, pre_gain = gains_ref[0:1, :], gains_ref[1:2, :]
+    post_gain, final_gain = gains_ref[2:3, :], gains_ref[3:4, :]
+    draft_load = pltpu.make_async_copy(
+        draft_ref.at[at.r * heads // reqs], draft_weight, draft_sem
+    )
+    draft_load.start()
     meet(at)
 
     own_copy = pltpu.make_async_copy(mlp_ref, weights.at[at.r], own_sem)
     own_copy.start()
     w_sent = []
-    for m in range(matrices):
+
+    def send_weights(m):
         for dy in range(1, at.chips):
             w_sent.append(
                 push(
@@ -265,6 +393,9 @@
             )
         )
 
+    for m in range(matrices - 1):
+        send_weights(m)
+
     def pass_on(m):
         for dy in range(1, at.chips):
             slot = at.req_from(dy, 0)
@@ -274,7 +405,10 @@
                 push(block, block, w_send.at[dy, 1, m], w_recv.at[slot, m], at.req(0, 1), at.u)
             )
 
-    sent = gather_units(at, attended_ref, attended_all, a_send, a_recv)
+    a_sent = start_gather(at, attended_ref, attended_all, a_send, a_recv)
+    a_sent += forward_gather(at, attended_all, a_send, a_recv)
+    sent = []
+    end_gather(at, attended_all, a_send, a_recv)
     columns = jnp.dot(
         attended_all[...].reshape(units * tree, depth),
         out_weight_ref[...],
@@ -299,40 +433,146 @@
         await_block(at, proj_recv.at[slot], p_send.at[dz, dx], p_recv.at[slot])
     projected = jnp.concatenate([proj_recv[j] for j in range(units)], axis=1)
     first = (
-        hidden_ref[...].astype(jnp.float32) + rms_scale(projected, attn_gain_ref[...])
+        hidden_ref[...].astype(jnp.float32) + rms_scale(projected, attn_gain)
     ).astype(jnp.bfloat16)
     first_ref[...] = first
-    normed_ref[...] = rms_scale(first, pre_gain_ref[...]).astype(jnp.bfloat16)
+    normed = rms_scale(first, pre_gain).astype(jnp.bfloat16)
+    normed_ref[...] = normed
+
+    pack_one[...] = pack_rows(accepted_ref, normed).astype(jnp.bfloat16)
+    path_first = pack_rows(accepted_ref, first)
+    sent += start_packed(at, pack_one, paths_one, l1_send, l1_recv)
+    sent += start_gather(at, normed_ref, normed_all, n_send, n_recv)
+    sent += spread_packed(at, paths_one, l1_send, l1_recv, m1_send, m1_recv)
+    send_weights(matrices - 1)
     pass_on(0)
-    sent += gather_units(at, normed_ref, normed_all, n_send, n_recv)
-    for m in range(1, matrices):
+    sent += forward_gather(at, normed_all, n_send, n_recv)
+    for m in range(1, matrices - 1):
         pass_on(m)
-
+    end_packed(at, paths_one, m1_send, m1_recv)
+    unpack_rows(paths_one, every)
     own_copy.wait()
+    rows, width = every.shape[0], depth // PACK
+    gate = jnp.dot(every[...], weights[at.r, 0], preferred_element_type=jnp.float32)
+    upward = jnp.dot(every[...], weights[at.r, 1], preferred_element_type=jnp.float32)
+    active = (jax.nn.gelu(gate, approximate=True) * upward).astype(jnp.bfloat16)
+    terms = [
+        dot_nt(active, weights[at.r, 2, chunk * width : (chunk + 1) * width, :]).astype(
+            jnp.bfloat16
+        )
+        for chunk in range(PACK)
+    ]
+    group = units * ACC
+    for k in range(reqs):
+        packed = jnp.zeros((group * PACK, width), jnp.float32)
+        for chunk in range(PACK):
+            packed = packed + lax.dot_general(
+                packed_places(group, chunk),
+                terms[chunk][k * group : (k + 1) * group, :],
+                (((0,), (0,)), ((), ())),
+                preferred_element_type=jnp.float32,
+            )
+        path_part[k] = packed.astype(jnp.bfloat16).reshape(path_part.shape[1:])
 
     def add_units(slot, start):
         rows = normed_all[...].reshape(units * tree, depth)
         gate = jnp.dot(rows, weights[slot, 0], preferred_element_type=jnp.float32)
         upward = jnp.dot(rows, weights[slot, 1], preferred_element_type=jnp.float32)
         active = (jax.nn.gelu(gate, approximate=True) * upward).astype(jnp.bfloat16)
-        terms = dot_nt(active, weights[slot, 2]).reshape(units, tree, depth)
-        part[...] = terms if start else part[...] + terms
-
-    add_units(at.r, True)
-
-    def one_chip(dy, carry):
-        @pl.when(dy > 0)
-        def _():
-            add_units(at.req_from(dy, 0), False)
-
-        slot = at.req_from(dy, 1)
-        for m in range(matrices):
-            await_block(at, weights.at[slot, m], w_send.at[0, 1, m], w_recv.at[slot, m])
-        add_units(slot, False)
-        return carry
-
-    lax.fori_loop(0, at.chips, one_chip, 0)
-
+        for chunk in range(PACK):
+            span = slice(chunk * width, (chunk + 1) * width)
+            terms = dot_nt(active, weights[slot, 2, span, :]).reshape(units, tree, width)
+            part[:, :, span] = terms if start else part[:, :, span] + terms
+
+    queue = [(dy, dc) for dy in range(at.chips) for dc in range(2)]
+
+    def next_units():
+        dy, dc = queue.pop(0)
+        slot = at.req_from(dy, dc)
+        if dc:
+            for m in range(matrices):
+                await_block(at, weights.at[slot, m], w_send.at[0, 1, m], w_recv.at[slot, m])
+        add_units(slot if dy or dc else at.r, not (dy or dc))
+
+    def end_units():
+        while queue:
+            next_units()
+
+    for dy, dc in at.req_peers():
+        peer = at.req(dy, dc)
+        sent.append(
+            push(
+                path_part.at[peer],
+                path_req.at[at.r],
+                e_send.at[dy, dc],
+                e_recv.at[at.r],
+                peer,
+                at.u,
+            )
+        )
+    path_req[at.r] = path_part[at.r]
+    end_gather(at, normed_all, n_send, n_recv)
+    next_units()
+    pass_on(matrices - 1)
+    for dy, dc in at.req_peers():
+        slot = at.req_from(dy, dc)
+        await_block(at, path_req.at[slot], e_send.at[dy, dc], e_recv.at[slot])
+    path_units[...] = jnp.sum(path_req[...].astype(jnp.float32), axis=0).astype(jnp.bfloat16)
+    for dz, dx in at.unit_peers():
+        peer = at.unit(dz, dx)
+        sent.append(
+            push(
+                path_units.at[peer],
+                path_in.at[at.u],
+                g_send.at[dz, dx],
+                g_recv.at[at.u],
+                at.r,
+                peer,
+            )
+        )
+    path_in[at.u] = path_units[at.u]
+    next_units()
+    for dz, dx in at.unit_peers():
+        slot = at.unit_from(dz, dx)
+        await_block(at, path_in.at[slot], g_send.at[dz, dx], g_recv.at[slot])
+    path_sum = jnp.sum(path_in[...].astype(jnp.float32), axis=0)
+    path_out = (path_first + packed_rms(path_sum, post_gain)).astype(jnp.bfloat16)
+    pack_two[...] = packed_rms(path_out.astype(jnp.float32), final_gain).astype(jnp.bfloat16)
+    sent += start_packed(at, pack_two, paths_two, l2_send, l2_recv)
+    sent += spread_packed(at, paths_two, l2_send, l2_recv, m2_send, m2_recv)
+    next_units()
+    end_packed(at, paths_two, m2_send, m2_recv)
+    unpack_rows(paths_two, every)
+
+    draft_load.wait()
+    share, columns_here = drafts.shape[2:]
+    if share == rows:
+        mine = every.at[:, :]
+    else:
+        start = pl.multiple_of(lax.rem(at.r * share, rows), share)
+        mine = every.at[pl.ds(start, share), :]
+    before = jnp.dot(mine[...], draft_weight[...], preferred_element_type=jnp.float32)
+    column = pl.multiple_of(at.u * columns_here, columns_here)
+    own = mine[:, pl.ds(column, columns_here)].astype(jnp.float32)
+    drafts[at.r, at.u] = (own + before * jax.nn.sigmoid(before)).astype(jnp.bfloat16)
+
+    block = drafts.at[at.r, at.u]
+    for dz in range(1, at.slow):
+        sent.append(push(block, block, h_send.at[dz, 0], h_recv.at[at.u], at.r, at.unit(dz, 0)))
+    for dx in range(1, at.fast):
+        sent.append(push(block, block, h_send.at[0, dx], h_recv.at[at.u], at.r, at.unit(0, dx)))
+    sent += forward_gather(at, drafts.at[at.r], h_send, h_recv)
+    end_gather(at, drafts.at[at.r], h_send, h_recv)
+    block = drafts.at[at.r]
+    for dy in range(1, at.chips):
+        sent.append(push(block, block, q_send.at[dy, 0], q_recv.at[at.r], at.req(dy, 0), at.u))
+    sent.append(push(block, block, q_send.at[0, 1], q_recv.at[at.r], at.req(0, 1), at.u))
+
+    end_units()
+
+    for copy in a_sent:
+        copy.wait_send()
+    sums_send = attended_all
     order = list(range(1, at.slow)) + [0]
     for dz in order:
         for dx in range(1, at.fast):
@@ -349,6 +589,12 @@
                     at.unit(0, dx),
                 )
             )
+    for dy in range(1, at.chips):
+        slot = at.req_from(dy, 0)
+        block = drafts.at[slot]
+        await_block(at, block, q_send.at[dy, 0], q_recv.at[slot])
+        sent.append(push(block, block, q_send.at[dy, 1], q_recv.at[slot], at.req(0, 1), at.u))
+
     for dz in order:
         target = at.unit(dz, 0)
         zt = target // at.fast
@@ -373,32 +619,32 @@
         zs = lax.rem(at.z + at.slow - dz, at.slow)
         await_block(at, sums_slow.at[zs], s_send.at[dz], s_recv.at[zs])
         total = total + sums_slow[zs].astype(jnp.float32)
-    tree_out = (
-        first_ref[...].astype(jnp.float32) + rms_scale(total, post_gain_ref[...])
+    tree_out_ref[...] = (
+        first_ref[...].astype(jnp.float32) + rms_scale(total, post_gain)
     ).astype(jnp.bfloat16)
-    tree_out_ref[...] = tree_out
-
-    ready = rms_scale(tree_out, final_gain_ref[...]).astype(jnp.bfloat16)
-    width = depth // PACK
-    row = lax.broadcasted_iota(jnp.int32, (PACK * ACC, tree), 0)
-    node = lax.broadcasted_iota(jnp.int32, (PACK * ACC, tree), 1)
-    packed = jnp.zeros((PACK * ACC, width), jnp.float32)
-    for chunk in range(PACK):
-        pick = jnp.zeros((PACK * ACC, tree), jnp.float32)
-        for i in range(ACC):
-            hit = (row == chunk * ACC + i) & (node == accepted_ref[0, i])
-            pick = jnp.where(hit, 1.0, pick)
-        packed = packed + jnp.dot(
-            pick.astype(jnp.bfloat16),
-            ready[:, chunk * width : (chunk + 1) * width],
-            preferred_element_type=jnp.float32,
-        )
-    path_ref[...] = packed.astype(jnp.bfloat16)
+    for dy in range(at.chips):
+        slot = at.req_from(dy, 1)
+        await_block(at, drafts.at[slot], q_send.at[dy, 1], q_recv.at[slot])
+    stores = [
+        pltpu.make_async_copy(
+            drafts.at[k, j],
+            drafts_ref.at[
+                k * share : (k + 1) * share, j * columns_here : (j + 1) * columns_here
+            ],
+            out_sem.at[k, j],
+        )
+        for k in range(reqs)
+        for j in range(units)
+    ]
+    for store in stores:
+        store.start()
+    for store in stores:
+        store.wait()
     for copy in sent + w_sent:
         copy.wait_send()
 
 
-def layer(attended, hidden, accepted, out_weight, mlp_weights, gains):
+def layer(attended, hidden, accepted, out_weight, mlp_weights, draft_weights, gains):
     reqs, units = lax.axis_size("req"), lax.axis_size("unit")
     slow, fast = split_unit(units)
     tree, depth = hidden.shape
@@ -407,16 +653,20 @@
     rows = (units, tree, depth)
     cols = (units, tree, out_weight.shape[1])
     matrices, _, width = mlp_weights.shape
+    heads, _, draft_width = draft_weights.shape
+    path_rows = reqs * units * ACC
+    block = (PACK * ACC, depth // PACK)
+    share = heads * path_rows // reqs
     return pl.pallas_call(
         layer_kernel,
         out_shape=(
             jax.ShapeDtypeStruct((tree, depth), bf16),
-            jax.ShapeDtypeStruct((PACK * ACC, depth // PACK), bf16),
+            jax.ShapeDtypeStruct((heads * path_rows, depth), bf16),
         ),
         in_specs=[pl.BlockSpec(memory_space=pltpu.SMEM)]
-        + [vmem] * 7
-        + [pl.BlockSpec(memory_space=pl.ANY)],
-        out_specs=(vmem, vmem),
+        + [vmem] * 4
+        + [pl.BlockSpec(memory_space=pl.ANY)] * 2,
+        out_specs=(vmem, pl.BlockSpec(memory_space=pl.ANY)),
         scratch_shapes=[
             pltpu.VMEM((reqs, matrices, depth, width), bf16),
             pltpu.VMEM(rows, bf16),
@@ -426,7 +676,6 @@
             pltpu.VMEM((tree, depth), bf16),
             pltpu.VMEM(rows, bf16),
             pltpu.VMEM(rows, jnp.float32),
-            pltpu.VMEM(rows, bf16),
             pltpu.VMEM((slow, fast, tree, depth), bf16),
             pltpu.VMEM((slow, tree, depth), bf16),
             dma(()),
@@ -442,143 +691,17 @@
             dma((slow, fast)),
             dma((slow,)),
             dma((slow,)),
-        ],
-        compiler_params=pltpu.CompilerParams(
-            collective_id=0, has_side_effects=True, vmem_limit_bytes=56 * MIB
-        ),
-        name="projection_and_feed_forward",
-    )(accepted, attended, hidden, out_weight, *[g[None, :] for g in gains], mlp_weights)
-
-
-def drafts_kernel(
-    path_ref,
-    weight_ref,
-    out_ref,
-    paths,
-    every,
-    weight,
-    drafts,
-    own_sem,
-    l_send,
-    l_recv,
-    m_send,
-    m_recv,
-    a_send,
-    a_recv,
-    q_send,
-    q_recv,
-):
-    at = Place()
-    reqs, units, packed, wide = paths.shape
-    heads = weight_ref.shape[0]
-    rows, depth = every.shape
-    share, width = drafts.shape[2:]
-    head = at.r * heads // reqs
-    load = pltpu.make_async_copy(weight_ref.at[head], weight, own_sem)
-    load.start()
-    meet(at)
-
-    sent = []
-    for dz, dx in at.unit_peers():
-        sent.append(
-            push(
-                path_ref,
-                paths.at[at.r, at.u],
-                l_send.at[dz, dx],
-                l_recv.at[at.u],
-                at.r,
-                at.unit(dz, dx),
-            )
-        )
-    paths[at.r, at.u] = path_ref[...]
-    for dz, dx in at.unit_peers():
-        slot = at.unit_from(dz, dx)
-        await_block(at, paths.at[at.r, slot], l_send.at[dz, dx], l_recv.at[slot])
-    for dy, dc in at.req_peers():
-        sent.append(
-            push(
-                paths.at[at.r],
-                paths.at[at.r],
-                m_send.at[dy, dc],
-                m_recv.at[at.r],
-                at.req(dy, dc),
-                at.u,
-            )
-        )
-    for dy, dc in at.req_peers():
-        slot = at.req_from(dy, dc)
-        await_block(at, paths.at[slot], m_send.at[dy, dc], m_recv.at[slot])
-    flat = paths[...].reshape(reqs * units * packed, wide)
-    row = lax.broadcasted_iota(jnp.int32, (rows, flat.shape[0]), 0)
-    place = lax.broadcasted_iota(jnp.int32, (rows, flat.shape[0]), 1)
-    base = row // ACC * packed + lax.rem(row, ACC)
-    for chunk in range(PACK):
-        pick = jnp.where(place == base + chunk * ACC, 1.0, 0.0).astype(jnp.bfloat16)
-        every[:, chunk * wide : (chunk + 1) * wide] = jnp.dot(
-            pick, flat, preferred_element_type=jnp.float32
-        ).astype(jnp.bfloat16)
-
-    load.wait()
-    if share == rows:
-        mine = every.at[:, :]
-    else:
-        start = pl.multiple_of(lax.rem(at.r * share, rows), share)
-        mine = every.at[pl.ds(start, share), :]
-    before = jnp.dot(mine[...], weight[...], preferred_element_type=jnp.float32)
-    own = mine[:, pl.ds(pl.multiple_of(at.u * width, width), width)].astype(jnp.float32)
-    drafts[at.r, at.u] = (own + before * jax.nn.sigmoid(before)).astype(jnp.bfloat16)
-
-    block = drafts.at[at.r, at.u]
-    for dz in range(1, at.slow):
-        sent.append(push(block, block, a_send.at[dz, 0], a_recv.at[at.u], at.r, at.unit(dz, 0)))
-    for dz in range(at.slow):
-        slot = at.unit_from(dz, 0)
-        block = drafts.at[at.r, slot]
-        if dz:
-            await_block(at, block, a_send.at[dz, 0], a_recv.at[slot])
-        for dx in range(1, at.fast):
-            sent.append(push(block, block, a_send.at[dz, dx], a_recv.at[slot], at.r, at.unit(0, dx)))
-    for dz in range(at.slow):
-        for dx in range(1, at.fast):
-            slot = at.unit_from(dz, dx)
-            await_block(at, drafts.at[at.r, slot], a_send.at[dz, dx], a_recv.at[slot])
-    block = drafts.at[at.r]
-    for dy in range(1, at.chips):
-        sent.append(push(block, block, q_send.at[dy, 0], q_recv.at[at.r], at.req(dy, 0), at.u))
-    for dy in range(at.chips):
-        slot = at.req_from(dy, 0)
-        block = drafts.at[slot]
-        if dy:
-            await_block(at, block, q_send.at[dy, 0], q_recv.at[slot])
-        sent.append(push(block, block, q_send.at[dy, 1], q_recv.at[slot], at.req(0, 1), at.u))
-    for dy in range(at.chips):
-        slot = at.req_from(dy, 1)
-        await_block(at, drafts.at[slot], q_send.at[dy, 1], q_recv.at[slot])
-    for k in range(reqs):
-        for j in range(units):
-            out_ref[k * share : (k + 1) * share, j * width : (j + 1) * width] = drafts[k, j]
-    for copy in sent:
-        copy.wait_send()
-
-
-def gather_drafts(path, draft_weights):
-    reqs, units = lax.axis_size("req"), lax.axis_size("unit")
-    slow, fast = split_unit(units)
-    heads, depth, width = draft_weights.shape
-    rows = reqs * units * ACC
-    share = heads * rows // reqs
-    bf16, dma = jnp.bfloat16, pltpu.SemaphoreType.DMA
-    vmem = pl.BlockSpec(memory_space=pltpu.VMEM)
-    return pl.pallas_call(
-        drafts_kernel,
-        out_shape=jax.ShapeDtypeStruct((heads * rows, depth), bf16),
-        in_specs=[vmem, pl.BlockSpec(memory_space=pl.ANY)],
-        out_specs=vmem,
-        scratch_shapes=[
-            pltpu.VMEM((reqs, units) + path.shape, bf16),
-            pltpu.VMEM((rows, depth), bf16),
-            pltpu.VMEM((depth, width), bf16),
-            pltpu.VMEM((reqs, units, share, width), bf16),
+            pltpu.VMEM(block, bf16),
+            pltpu.VMEM((reqs, units) + block, bf16),
+            pltpu.VMEM(block, bf16),
+            pltpu.VMEM((reqs, units) + block, bf16),
+            pltpu.VMEM((path_rows, depth), bf16),
+            pltpu.VMEM((reqs, units) + block, bf16),
+            pltpu.VMEM((reqs, units) + block, bf16),
+            pltpu.VMEM((units,) + block, bf16),
+            pltpu.VMEM((units,) + block, bf16),
+            pltpu.VMEM((depth, draft_width), bf16),
+            pltpu.VMEM((reqs, units, share, draft_width), bf16),
             dma(()),
             dma((slow, fast)),
             dma((units,)),
@@ -588,12 +711,21 @@
             dma((units,)),
             dma((reqs // 2, 2)),
             dma((reqs,)),
+            dma((reqs // 2, 2)),
+            dma((reqs,)),
+            dma((slow, fast)),
+            dma((units,)),
+            dma((slow, fast)),
+            dma((units,)),
+            dma((reqs // 2, 2)),
+            dma((reqs,)),
+            dma((reqs, units)),
         ],
         compiler_params=pltpu.CompilerParams(
-            collective_id=1, has_side_effects=True, vmem_limit_bytes=48 * MIB
+            collective_id=0, has_side_effects=True, vmem_limit_bytes=56 * MIB
         ),
-        name="draft_heads",
-    )(path, draft_weights)
+        name="projection_feed_forward_drafts",
+    )(accepted, attended, hidden, out_weight, jnp.stack(gains), mlp_weights, draft_weights)
 
 
 def sum_kernel(own_ref, out_ref, unit_parts, group, req_parts, u_send, u_recv, r_send, r_recv):
@@ -685,7 +817,7 @@
         span = slice(c * chunk, (c + 1) * chunk)
         products = dot_nt(drafts_ref[...], emb_ref[span, :])
         logits = SOFTCAP * jnp.tanh(products * (1.0 / SOFTCAP))
-        logits_ref[:, span] = logits
+        logits_ref[:, span] = logits.astype(jnp.bfloat16)
         keep = allowed_ids(start, end, first_id + step * tile + c * chunk, logits.shape)
         terms = jnp.where(keep, jnp.exp(logits), 0.0)
         part = terms[:, :128]
@@ -701,7 +833,7 @@
     keep = allowed_ids(
         start_ref[...], end_ref[...], first_id + pl.program_id(0) * tile, logits_ref.shape
     )
-    values = jnp.where(keep, logits_ref[...] - logs_ref[...], 0.0).astype(jnp.bfloat16)
+    values = jnp.where(keep, logits_ref[...].astype(jnp.float32) - logs_ref[...], 0.0).astype(jnp.bfloat16)
     out_ref[...] = values.reshape(out_ref.shape)
 
 
@@ -717,7 +849,7 @@
         functools.partial(logits_kernel, min(256, tile)),
         grid=(vocab // tile,),
         out_shape=(
-            jax.ShapeDtypeStruct((count, vocab), jnp.float32),
+            jax.ShapeDtypeStruct((count, vocab), jnp.bfloat16),
             jax.ShapeDtypeStruct((count, 128), jnp.float32),
         ),
         in_specs=[
@@ -733,7 +865,7 @@
         compiler_params=pltpu.CompilerParams(vmem_limit_bytes=56 * MIB),
         cost_estimate=pl.CostEstimate(
             flops=2 * count * depth * vocab,
-            bytes_accessed=2 * depth * vocab + 4 * count * vocab,
+            bytes_accessed=2 * depth * vocab + 2 * count * vocab,
             transcendentals=2 * count * vocab,
         ),
         name="vocabulary_logits",
@@ -747,7 +879,7 @@
         out_specs=pl.BlockSpec((HEADS, rows, tile), lambda i: (0, 0, i)),
         compiler_params=pltpu.CompilerParams(vmem_limit_bytes=40 * MIB),
         cost_estimate=pl.CostEstimate(
-            flops=2 * count * vocab, bytes_accessed=6 * count * vocab, transcendentals=0
+            flops=2 * count * vocab, bytes_accessed=4 * count * vocab, transcendentals=0
         ),
         name="log_probabilities",
     )(logits, jnp.log(totals)[:, None], starts, ends)
@@ -773,8 +905,9 @@
 ):
     attended = attend(tree_q, tree_kv, kv_cache, cache_lengths, tree_parents)
     gains = (attn_post_gain, ff_pre_gain, ff_post_gain, final_gain)
-    tree_out, path = layer(attended, hidden, accepted, out_weight, mlp_weights, gains)
-    drafts = gather_drafts(path, draft_weights)
+    tree_out, drafts = layer(
+        attended, hidden, accepted, out_weight, mlp_weights, draft_weights, gains
+    )
     return (tree_out, vocabulary(drafts, embedding, tenant_ranges))
 
 

time: 222 us -> 218 us (0.982)
  Pallas kernels: 202 us -> 199 us
    pallas_call x1 -> x0, Pallas kernels: 41.6 us -> none  [gather_drafts(): pl.pallas_call(drafts_kernel, out_shape=jax.ShapeDtypeStruct((heads * row...]
    pallas_call x1, Pallas kernels: 107 us -> 147 us  [layer(): pl.pallas_call(layer_kernel, out_shape=(jax.ShapeDtypeStruct((tree, depth...]
    pallas_call x1, Pallas kernels: 12.7 us -> 7.44 us  [vocabulary(): pl.pallas_call(finish_kernel, grid=(vocab // tile,), out_shape=jax.ShapeD...]
    broadcast_in_dim x4 -> x0, local copies, waits for them, and re-layouts: 5.13 us -> none  [layer(): g[None, :]]
    pallas_call x1, Pallas kernels: 10.1 us -> 12.9 us  [sum_over_devices(): pl.pallas_call(sum_kernel, out_shape=jax.ShapeDtypeStruct(block, f32), in...]
    another operation x0 -> x4, local copies, waits for them, and re-layouts: none -> 2.77 us  [layer(): jnp.stack(gains)]
    unnamed x20 -> x18, local copies, waits for them, and re-layouts: 7.91 us -> 9.26 us
where the time goes in v3:
time: 218 us
  Pallas kernels  199 us (91%)
  local copies, waits for them, and re-layouts  15.5 us (7%)
    pallas_call x1, Pallas kernels, layer(): pl.pallas_call(layer_kernel, out_shape=(jax.ShapeDtypeStruct((tree, depth...  147 us
    pallas_call x1, Pallas kernels, vocabulary(): pl.pallas_call(functools.partial(logits_kernel, min(256, tile)), grid=(vo...  27.6 us
    pallas_call x1, Pallas kernels, sum_over_devices(): pl.pallas_call(sum_kernel, out_shape=jax.ShapeDtypeStruct(block, f32), in...  12.9 us
    unnamed x18, local copies, waits for them, and re-layouts  9.26 us
    pallas_call x1, Pallas kernels, vocabulary(): pl.pallas_call(finish_kernel, grid=(vocab // tile,), out_shape=jax.ShapeD...  7.44 us

profile of v3, /device:TPU:0, one launch (start us, length us, event | category | flops | bytes accessed | tf_op | source)
XLA Modules:
  0.0 217.7 jit_solution(12954498979193661635)
XLA Ops:
  1.3 0.7 stack.15
  2.0 0.7 stack.16
  2.7 0.7 stack.17
  3.4 0.7 stack.18
  4.0 0.6 pad_maximum_fusion.gains_ref
  4.7 0.8 copy.23
  5.5 1.1 fusion.1
  6.7 2.2 %copy-done.1 = bf16[1,2,2,2048,256]{4,3,2,1,0:T(8,128)(2,1)S(1)} copy-done((bf16[1,2,2,2048,256]{4,3,2,1,0:T(8,128)(2,1)S(1)}, bf16[1,2,2,2048,256]{4,3,2,1,0:T(8,128)(2,1)}, u32[]{:S(2)}) %copy-start.1) | copy-done | bytes 4194328
  8.9 0.9 copy-done.5
  9.8 0.7 copy-done.6
  10.4 3.6 %tree_attention.1.attended_ref = bf16[48,2048]{1,0:T(8,128)(2,1)S(1)} custom-call(s32[1]{0:T(128)S(6)} %copy.30.length_ref, s32[1,48]{1,0:T(1,128)S(1)} %copy-done.6, bf16[48,2048]{1,0:T(8,128)(2,1)S(1)} %copy-done.5, bf16[48,512]{1,0:T(8,128)(2,1)S(1)} %get-tuple-element.15.tk_ref, bf16[48,512]{1,0:T(8,128)(2,1)S(1)} %get-tuple-element.14.tv_ref, ...), custom_call_target="tpu_custom_call" | custom-call | flops 805306368 | bytes 8388608 | tf_op jit(solution)/shard_map/tree_attention/pallas_call | solution.py:84
  14.0 0.0 copy-start.4
  14.1 0.7 copy-done.4
  14.7 0.9 fusion
  15.6 147.4 %projection_feed_forward_drafts.1 = (bf16[48,2048]{1,0:T(8,128)(2,1)}, bf16[512,2048]{1,0:T(8,128)(2,1)}) custom-call(s32[1,4]{1,0:T(1,128)} %accepted_ref.1, bf16[48,2048]{1,0:T(8,128)(2,1)} %copy-done.4, bf16[48,2048]{1,0:T(8,128)(2,1)} %hidden_ref.1, bf16[2048,256]{1,0:T(8,128)(2,1)} %out_weight_ref.1, bf16[4,2048]{1,0:T(4,128)(2,1)} %pad_maximum_fusion.gains_ref, ...), custom_call_target="tpu_custom_call" | custom-call | tf_op jit(solution)/shard_map/projection_feed_forward_drafts/pallas_call | solution.py:660
  163.1 27.6 %vocabulary_logits.1 = (bf16[512,8192]{1,0:T(8,128)(2,1)}, f32[512,128]{1,0:T(8,128)}) custom-call(bf16[512,2048]{1,0:T(8,128)(2,1)} %get-tuple-element.7.drafts_ref, bf16[8192,2048]{1,0:T(8,128)(2,1)} %emb_ref.1, s32[512,1]{1,0:T(8,128)} %get-tuple-element.11.start_ref, s32[512,1]{1,0:T(8,128)} %get-tuple-element.10.end_ref), custom_call_target="tpu_custom_call" | custom-call | flops 17179869184 | bytes 41943040 | tf_op jit(solution)/shard_map/vocabulary_logits/pallas_call | solution.py:848
  190.7 1.1 reduce_sum.9
  191.8 0.6 pad_bitcast_fusion.own_ref
  192.4 12.9 %sum_of_totals.1 = f32[8,128]{1,0:T(8,128)} custom-call(f32[8,128]{1,0:T(8,128)} %pad_bitcast_fusion.own_ref), custom_call_target="tpu_custom_call" | custom-call | tf_op jit(solution)/shard_map/sum_of_totals/pallas_call | solution.py:779
  205.3 0.7 slice_log_fusion
  206.0 0.2 copy.24.logs_ref
  206.2 3.4 %copy-done = bf16[512,8192]{1,0:T(8,128)(2,1)S(1)} copy-done((bf16[512,8192]{1,0:T(8,128)(2,1)S(1)}, bf16[512,8192]{1,0:T(8,128)(2,1)}, u32[]{:S(2)}) %copy-start) | copy-done | bytes 8388632
  209.5 7.4 %log_probabilities.1 = bf16[4,128,8192]{2,1,0:T(8,128)(2,1)} custom-call(bf16[512,8192]{1,0:T(8,128)(2,1)S(1)} %copy-done, f32[512,1]{1,0:T(8,128)S(1)} %copy.24.logs_ref, s32[512,1]{1,0:T(8,128)S(1)} %copy-done.3, s32[512,1]{1,0:T(8,128)S(1)} %copy-done.2), custom_call_target="tpu_custom_call" | custom-call | flops 8388608 | bytes 16777216 | tf_op jit(solution)/shard_map/log_probabilities/pallas_call | solution.py:874
  217.0 0.7 copy.31
  (13 shorter events, 0.1 us)
Async XLA Ops:
  6.7 2.2 %copy-start.1 = (bf16[1,2,2,2048,256]{4,3,2,1,0:T(8,128)(2,1)S(1)}, bf16[1,2,2,2048,256]{4,3,2,1,0:T(8,128)(2,1)}, u32[]{:S(2)}) copy-start(bf16[1,2,2,2048,256]{4,3,2,1,0:T(8,128)(2,1)} %cache_ref.1) | copy-start | bytes 12582916
  8.9 0.9 copy-start.5
  9.8 0.7 copy-start.6
  14.0 0.7 copy-start.4
  163.1 43.1 %copy-start.2 = (s32[512,1]{1,0:T(8,128)S(1)}, s32[512,1]{1,0:T(8,128)}, u32[]{:S(2)}) copy-start(s32[512,1]{1,0:T(8,128)} %get-tuple-element.10.end_ref) | copy-start | bytes 6148
  163.1 43.1 %copy-start.3 = (s32[512,1]{1,0:T(8,128)S(1)}, s32[512,1]{1,0:T(8,128)}, u32[]{:S(2)}) copy-start(s32[512,1]{1,0:T(8,128)} %get-tuple-element.11.start_ref) | copy-start | bytes 6148
  206.2 3.4 %copy-start = (bf16[512,8192]{1,0:T(8,128)(2,1)S(1)}, bf16[512,8192]{1,0:T(8,128)(2,1)}, u32[]{:S(2)}) copy-start(bf16[512,8192]{1,0:T(8,128)(2,1)} %get-tuple-element.8.logits_ref) | copy-start | bytes 25165828
  209.5 7.4 %copy-start.7 = (bf16[48,2048]{1,0:T(8,128)(2,1)S(1)}, bf16[48,2048]{1,0:T(8,128)(2,1)}, u32[]{:S(2)}) copy-start(bf16[48,2048]{1,0:T(8,128)(2,1)} %get-tuple-element.18) | copy-start | bytes 589828
